TPU v7x, 256 devices: a whole 4x4x8 slice. The times are simulated.
256 devices in a mesh: pipe: 8 (over x, core), expert: 32 (over y, z).
Axes of the slice: x: 4, y: 4, z: 8, core: 2. Of those that a mesh axis runs over, the one named last changes fastest.
Arguments:
- tokens: bfloat16 [8, 4096, 3584], P('pipe', 'expert'), may hold values from -6 to 6
- expert_ids: int32 [8, 4096, 1], P('pipe', 'expert'), may hold values from 0 to 3; in each aligned block of 128 rows (0 to 127, 128 to 255, ..., all dimensions but the last counted through in order) at most 33 rows name the same one
- route_weight: bfloat16 [8, 4096, 1], P('pipe', 'expert'), may hold values from 0.049804688 to 0.5
- cotangent: bfloat16 [8, 4096, 3584], P('pipe', 'expert'), may hold values from -1.5 to 1.5
- w_gate: bfloat16 [8, 3584, 4096], P('pipe', None, 'expert'), as said below
- w_up: bfloat16 [8, 3584, 4096], P('pipe', None, 'expert'), as said below
- w_down: bfloat16 [8, 4096, 3584], P('pipe', 'expert'), as said below
Outputs:
- token_grad: bfloat16 [8, 4096, 3584], P('pipe', 'expert')
- route_grad: bfloat16 [8, 4096, 1], P('pipe', 'expert')
- grad_gate: bfloat16 [8, 3584, 4096], P('pipe', None, 'expert')
- grad_up: bfloat16 [8, 3584, 4096], P('pipe', None, 'expert')
- grad_down: bfloat16 [8, 4096, 3584], P('pipe', 'expert')
Inputs may be any that keep to these rules, and one draw needn't show every extreme that they name: `expert_ids`: each token names one expert; among one device's 128 tokens no expert is named more than 33 times, a bound that some block reaches. `w_gate`: the copies of ranks 2j and 2j + 1 are equal. `w_up`: the copies of ranks 2j and 2j + 1 are equal. `w_down`: the copies of ranks 2j and 2j + 1 are equal.
All inputs are finite; a program needn't handle non-finite values.
Results may differ from a plain program's by a relative error of at most 0.0065.
Values may be sent and summed in bfloat16 or wider, within the bound.
A program may use at most 128 MiB of HBM per device.

v0:
```python
import jax
import jax.numpy as jnp
from jax import lax
from jax.sharding import PartitionSpec as P

EXPERTS = 4


def partner_2(value, axis, apart):
    mask = 2**apart
    pairs = [(source, source ^ mask) for source in range(lax.axis_size(axis))]
    return lax.ppermute(value, axis, pairs)


def make_slots(block_ids, experts, capacity):
    flat_ids = block_ids.reshape(-1)
    onehot = (flat_ids[:, None] == jnp.arange(experts, dtype=jnp.int32)[None, :]).astype(jnp.int32)
    running = jnp.cumsum(onehot, axis=0) * onehot
    target_slot = flat_ids * capacity + jnp.sum(running, axis=1) - 1
    positions = jnp.arange(flat_ids.shape[0], dtype=jnp.int32)
    source_row = jnp.full((experts * capacity,), -1, jnp.int32).at[target_slot].set(positions)
    return (source_row, target_slot)


def pack_rows(source_row, values, top_count):
    filled = source_row >= 0
    picked = values[jnp.maximum(source_row, 0) // top_count]
    return jnp.where(filled[:, None], picked, jnp.zeros_like(picked))


def pack_weights(source_row, route_block):
    filled = source_row >= 0
    picked = route_block.reshape(-1)[jnp.maximum(source_row, 0)]
    return jnp.where(filled, picked, jnp.zeros_like(picked))


def contract_rows(left, right):
    return lax.dot_general(
        left, right, (((0,), (0,)), ((), ())), preferred_element_type=jnp.float32
    )


def contract_cols(left, right):
    return lax.dot_general(
        left, right, (((1,), (1,)), ((), ())), preferred_element_type=jnp.float32
    )


def expert_forward(recv_rows, gate_weight, up_weight, down_weight):
    gate_pre = jnp.dot(recv_rows, gate_weight, preferred_element_type=jnp.float32)
    up_pre = jnp.dot(recv_rows, up_weight, preferred_element_type=jnp.float32)
    gate_sig = jax.nn.sigmoid(gate_pre)
    hidden = (gate_pre * gate_sig * up_pre).astype(jnp.bfloat16)
    expert_out = jnp.dot(hidden, down_weight, preferred_element_type=jnp.float32)
    return (gate_pre, up_pre, hidden, expert_out)


def expert_backward(
    recv_rows, slot_weight, cot_rows, saved_state, gate_weight, up_weight, down_weight
):
    gate_pre, up_pre, hidden, expert_out = saved_state
    cot_wide = cot_rows.astype(jnp.float32)
    scaled = (slot_weight.astype(jnp.float32)[:, None] * cot_wide).astype(jnp.bfloat16)
    slot_grad = jnp.sum(expert_out * cot_wide, axis=1).astype(jnp.bfloat16)
    hidden_grad = contract_cols(scaled, down_weight)
    gate_sig = jax.nn.sigmoid(gate_pre)
    grad_gate_pre = (hidden_grad * up_pre * gate_sig * (1.0 + gate_pre * (1.0 - gate_sig))).astype(
        jnp.bfloat16
    )
    grad_up_pre = (hidden_grad * gate_pre * gate_sig).astype(jnp.bfloat16)
    row_grad = (
        contract_cols(grad_gate_pre, gate_weight) + contract_cols(grad_up_pre, up_weight)
    ).astype(jnp.bfloat16)
    gate_term = contract_rows(recv_rows, grad_gate_pre).astype(jnp.bfloat16)
    up_term = contract_rows(recv_rows, grad_up_pre).astype(jnp.bfloat16)
    down_term = contract_rows(hidden, scaled).astype(jnp.bfloat16)
    return (row_grad, slot_grad, gate_term, up_term, down_term)


def pair_sum(local_term, other_term):
    return (local_term.astype(jnp.float32) + other_term.astype(jnp.float32)).astype(jnp.bfloat16)


def shards(tokens, expert_ids, route_weight, cotangent, w_gate, w_up, w_down):
    devices_count = lax.axis_size("expert")
    group_size = devices_count // EXPERTS
    tok_count = tokens.shape[1]
    feature_count = tokens.shape[2]
    top_count = expert_ids.shape[2]
    capacity = min(tok_count, tok_count * top_count // EXPERTS + max(1, tok_count // 128))
    gate_weight = w_gate[0]
    up_weight = w_up[0]
    down_weight = w_down[0]
    source_row, target_slot = make_slots(expert_ids[0], EXPERTS, capacity)
    row_send = jnp.repeat(
        pack_rows(source_row, tokens[0], top_count).reshape(EXPERTS, capacity, feature_count),
        group_size,
        axis=0,
    )
    cot_send = jnp.repeat(
        pack_rows(source_row, cotangent[0], top_count).reshape(EXPERTS, capacity, feature_count),
        group_size,
        axis=0,
    )
    weight_send = jnp.repeat(
        pack_weights(source_row, route_weight[0]).reshape(EXPERTS, capacity), group_size, axis=0
    )
    row_recv, weight_recv, cot_recv = (
        lax.all_to_all(row_send, "expert", split_axis=0, concat_axis=0, tiled=True),
        lax.all_to_all(weight_send, "expert", split_axis=0, concat_axis=0, tiled=True),
        lax.all_to_all(cot_send, "expert", split_axis=0, concat_axis=0, tiled=True),
    )
    recv_rows = row_recv.reshape(devices_count * capacity, feature_count)
    saved_state = expert_forward(recv_rows, gate_weight, up_weight, down_weight)
    row_grad, slot_grad, gate_term, up_term, down_term = expert_backward(
        recv_rows,
        weight_recv.reshape(-1),
        cot_recv.reshape(devices_count * capacity, feature_count),
        saved_state,
        gate_weight,
        up_weight,
        down_weight,
    )
    back_rows, back_weight = (
        lax.all_to_all(
            row_grad.reshape(devices_count, capacity, feature_count),
            "expert",
            split_axis=0,
            concat_axis=0,
            tiled=True,
        ),
        lax.all_to_all(
            slot_grad.reshape(devices_count, capacity),
            "expert",
            split_axis=0,
            concat_axis=0,
            tiled=True,
        ),
    )
    expert_index = target_slot // capacity
    slot_index = target_slot % capacity
    grouped = back_rows.reshape(EXPERTS, group_size, capacity, feature_count)
    picked = grouped[expert_index, :, slot_index].astype(jnp.float32)
    token_grad = jnp.sum(
        picked.reshape(tok_count, top_count, group_size, feature_count), axis=(1, 2)
    ).astype(jnp.bfloat16)
    weight_parts = back_weight.reshape(EXPERTS, group_size, capacity)[
        expert_index, :, slot_index
    ].astype(jnp.float32)
    route_grad = jnp.sum(weight_parts, axis=1).astype(jnp.bfloat16).reshape(tok_count, top_count)
    partner = partner_2((gate_term, up_term, down_term), "pipe", 0)
    grad_gate = pair_sum(gate_term, partner[0])
    grad_up = pair_sum(up_term, partner[1])
    grad_down = pair_sum(down_term, partner[2])
    return (token_grad[None], route_grad[None], grad_gate[None], grad_up[None], grad_down[None])


def solution(mesh):
    in_specs = (
        P("pipe", "expert", None),
        P("pipe", "expert", None),
        P("pipe", "expert", None),
        P("pipe", "expert", None),
        P("pipe", None, "expert"),
        P("pipe", None, "expert"),
        P("pipe", "expert", None),
    )
    out_specs = (
        P("pipe", "expert", None),
        P("pipe", "expert", None),
        P("pipe", None, "expert"),
        P("pipe", None, "expert"),
        P("pipe", "expert", None),
    )
    return jax.shard_map(shards, mesh=mesh, in_specs=in_specs, out_specs=out_specs, check_vma=False)
```

profile of v0, /device:TPU:32, one launch (start us, length us, event | category | flops | bytes accessed | tf_op | source)
XLA Modules:
  0.0 770.3 jit_solution(5540356278690718913)
XLA Ops:
  0.7 0.9 fusion.18
  1.5 0.2 reduce_window_sum.11
  1.7 0.8 select_reduce_fusion
  2.5 0.7 fusion.25
  3.2 1.0 scatter_custom_fusion
  4.2 1.9 gather_fusion
  6.3 0.6 copy.20
  6.9 11.4 %all-to-all-start = ((bf16[32,1,33]{2,1,0:T(2,128)(2,1)}), bf16[32,1,33]{2,1,0:T(2,128)(2,1)S(1)}, u32[]{:S(2)}, u32[]{:S(2)}) async-start(bf16[32,1,33]{2,1,0:T(2,128)(2,1)} %copy.20), calls=%async_computation | async-start | bytes 32768 | tf_op jit(solution)/shard_map/all_to_all | solution.py:110
  18.3 3.4 gather_fusion.2
  21.7 1.3 gather.23
  23.0 1.1 gather_fusion.1
  24.2 1.3 gather.21
  25.5 1.8 broadcast_select_fusion.1
  27.3 0.6 broadcast_in_dim.58
  28.0 212.1 %all_to_all.30 = bf16[32,33,3584]{2,1,0:T(8,128)(2,1)} all-to-all(bf16[32,33,3584]{2,1,0:T(8,128)(2,1)S(1)} %bitcast.70), channel_id=1, replica_groups=mesh['pipe'=8,'expert'=32] {'expert'}, dimensions={0} | all-to-all | bytes 15138816 | tf_op jit(solution)/shard_map/all_to_all | solution.py:111
  240.0 4.3 broadcast_in_dim.59
  244.3 5.7 all-to-all-start.2
  250.1 10.5 %multiply_convert_fusion = bf16[32,33,3584]{2,1,0:T(8,128)(2,1)} fusion(f32[32,33]{1,0:T(8,128)S(1)} %bitcast.72, bf16[32,33,3584]{2,1,0:T(8,128)(2,1)} %all_to_all.30), kind=kLoop, calls=%fused_computation.8 | loop fusion | flops 11354112 | bytes 15143040 | tf_op jit(solution)/shard_map/convert_element_type | solution.py:63
  260.6 8.0 %convert_element_type.119 = bf16[1056,3584]{1,0:T(8,128)(2,1)} reshape(bf16[32,33,3584]{2,1,0:T(8,128)(2,1)} %multiply_convert_fusion) | data formatting | bytes 15138816 | tf_op jit(solution)/shard_map/convert_element_type | solution.py:63
  268.6 6.1 fusion.16
  274.7 183.9 %all-to-all-done.2 = bf16[32,33,3584]{2,1,0:T(8,128)(2,1)} async-done(((bf16[32,33,3584]{2,1,0:T(8,128)(2,1)}), bf16[32,33,3584]{2,1,0:T(8,128)(2,1)}, u32[]{:S(2)}, u32[]{:S(2)}) %all-to-all-start.2) | async-done | bytes 7569440 | tf_op jit(solution)/shard_map/all_to_all | solution.py:109
  458.6 7.9 %reshape.201 = bf16[1056,3584]{1,0:T(8,128)(2,1)} reshape(bf16[32,33,3584]{2,1,0:T(8,128)(2,1)} %all-to-all-done.2) | data formatting | bytes 15138816 | tf_op jit(solution)/shard_map/reshape | solution.py:113
  466.5 5.4 fusion.10
  471.9 3.0 multiply_convert_fusion.5
  474.9 10.2 %reshape.206 = f32[1056,3584]{1,0:T(8,128)} reshape(bf16[32,33,3584]{2,1,0:T(8,128)(2,1)} %all_to_all.30) | data formatting | bytes 22708224 | tf_op jit(solution)/shard_map/convert_element_type | solution.py:62
  485.1 7.5 fusion.4
  492.7 0.7 convert_element_type.147
  493.4 6.9 all-to-all-start.4
  500.3 3.4 fusion.8
  503.7 6.1 fusion
  509.9 7.9 %reshape.202 = bf16[32,33,3584]{2,1,0:T(8,128)(2,1)} reshape(bf16[1056,3584]{1,0:T(8,128)(2,1)} %fusion) | data formatting | bytes 15138816 | tf_op jit(solution)/shard_map/reshape | solution.py:126
  517.8 10.0 %all-to-all-start.3 = ((bf16[32,33,3584]{2,1,0:T(8,128)(2,1)}), bf16[32,33,3584]{2,1,0:T(8,128)(2,1)}, u32[]{:S(2)}, u32[]{:S(2)}) async-start(bf16[32,33,3584]{2,1,0:T(8,128)(2,1)} %reshape.202), calls=%async_computation.3 | async-start | bytes 18350080 | tf_op jit(solution)/shard_map/all_to_all | solution.py:125
  527.8 0.1 reshape.207
  527.9 5.5 convolution_convert_fusion
  533.6 6.5 convolution_convert_fusion.1
  540.1 0.7 collective-permute-start
  540.8 6.7 fusion.3
  547.5 0.1 collective-permute-start.2
  547.6 0.1 copy.24
  547.7 1.1 gather_fusion.4
  548.8 0.6 reduce_sum.48
  549.5 2.3 fusion.6
  551.8 2.6 fusion.5
  554.4 2.3 fusion.7
  556.8 188.3 %all-to-all-done.3 = bf16[32,33,3584]{2,1,0:T(8,128)(2,1)} async-done(((bf16[32,33,3584]{2,1,0:T(8,128)(2,1)}), bf16[32,33,3584]{2,1,0:T(8,128)(2,1)}, u32[]{:S(2)}, u32[]{:S(2)}) %all-to-all-start.3) | async-done | bytes 7569440 | tf_op jit(solution)/shard_map/all_to_all | solution.py:125
  745.1 9.0 %copy.22 = bf16[4,8,33,3584]{3,1,2,0:T(8,128)(2,1)} copy(bf16[4,8,33,3584]{3,2,1,0:T(8,128)(2,1)} %bitcast.14) | data formatting | bytes 15138816 | tf_op jit(solution)/shard_map/reshape | solution.py:142
  754.0 7.1 gather_fusion.3
  761.2 8.9 %reduce_sum.46 = bf16[128,3584]{1,0:T(8,128)(2,1)} reduce(bf16[128,8,3584]{2,1,0:T(8,128)(2,1)} %gather_fusion.3, bf16[]{:T(256)} %constant.56.clone.1), dimensions={1}, to_apply=%region_3.4 | reduce | flops 3211264 | bytes 8257538 | tf_op jit(solution)/shard_map/reduce_sum | solution.py:144
  (36 shorter events, 0.4 us)
Async XLA Ops:
  0.6 471.3 %copy-start = (bf16[1,3584,128]{2,1,0:T(8,128)(2,1)S(1)}, bf16[1,3584,128]{2,1,0:T(8,128)(2,1)}, u32[]{:S(2)}) copy-start(bf16[1,3584,128]{2,1,0:T(8,128)(2,1)} %param.12) | copy-start | bytes 2752516
  0.6 22.4 %copy-start.1 = (bf16[1,128,3584]{2,1,0:T(8,128)(2,1)S(1)}, bf16[1,128,3584]{2,1,0:T(8,128)(2,1)}, u32[]{:S(2)}) copy-start(bf16[1,128,3584]{2,1,0:T(8,128)(2,1)} %param.10) | copy-start | bytes 2752516
  6.9 20.4 %all-to-all-start = ((bf16[32,1,33]{2,1,0:T(2,128)(2,1)}), bf16[32,1,33]{2,1,0:T(2,128)(2,1)S(1)}, u32[]{:S(2)}, u32[]{:S(2)}) async-start(bf16[32,1,33]{2,1,0:T(2,128)(2,1)} %copy.20), calls=%async_computation | async-start | bytes 32768 | tf_op jit(solution)/shard_map/all_to_all | solution.py:110
  244.3 214.3 %all-to-all-start.2 = ((bf16[32,33,3584]{2,1,0:T(8,128)(2,1)}), bf16[32,33,3584]{2,1,0:T(8,128)(2,1)}, u32[]{:S(2)}, u32[]{:S(2)}) async-start(bf16[32,33,3584]{2,1,0:T(8,128)(2,1)} %bitcast.69), calls=%async_computation.2 | async-start | bytes 18350080 | tf_op jit(solution)/shard_map/all_to_all | solution.py:109
  260.6 8.0 %copy-start.5 = (bf16[1,128,3584]{2,1,0:T(8,128)(2,1)S(1)}, bf16[1,128,3584]{2,1,0:T(8,128)(2,1)}, u32[]{:S(2)}) copy-start(bf16[1,128,3584]{2,1,0:T(8,128)(2,1)} %param.13) | copy-start | bytes 2752516
  274.7 191.7 %copy-start.6 = (bf16[1,3584,128]{2,1,0:T(8,128)(2,1)S(1)}, bf16[1,3584,128]{2,1,0:T(8,128)(2,1)}, u32[]{:S(2)}) copy-start(bf16[1,3584,128]{2,1,0:T(8,128)(2,1)} %param.11) | copy-start | bytes 2752516
  466.5 5.4 copy-start.2
  466.5 5.5 copy-start.9
  474.9 10.2 %copy-start.3 = (bf16[1056,128]{1,0:T(8,128)(2,1)}, bf16[1056,128]{1,0:T(8,128)(2,1)S(1)}, u32[]{:S(2)}) copy-start(bf16[1056,128]{1,0:T(8,128)(2,1)S(1)} %get-tuple-element.7) | copy-start | bytes 811012
  493.4 24.4 %all-to-all-start.4 = ((bf16[32,1,33]{2,1,0:T(2,128)(2,1)}), bf16[32,1,33]{2,1,0:T(2,128)(2,1)S(1)}, u32[]{:S(2)}, u32[]{:S(2)}) async-start(bf16[32,1,33]{2,1,0:T(2,128)(2,1)} %convert_element_type.147), calls=%async_computation.4 | async-start | bytes 32768 | tf_op jit(solution)/shard_map/all_to_all | solution.py:132
  517.8 10.2 %copy-start.8 = (bf16[1056,128]{1,0:T(8,128)(2,1)S(1)}, bf16[1056,128]{1,0:T(8,128)(2,1)}, u32[]{:S(2)}) copy-start(bf16[1056,128]{1,0:T(8,128)(2,1)} %get-tuple-element.9) | copy-start | bytes 811012
  517.8 227.3 %all-to-all-start.3 = ((bf16[32,33,3584]{2,1,0:T(8,128)(2,1)}), bf16[32,33,3584]{2,1,0:T(8,128)(2,1)}, u32[]{:S(2)}, u32[]{:S(2)}) async-start(bf16[32,33,3584]{2,1,0:T(8,128)(2,1)} %reshape.202), calls=%async_computation.3 | async-start | bytes 18350080 | tf_op jit(solution)/shard_map/all_to_all | solution.py:125
  527.7 5.9 copy-start.7
  533.5 7.3 copy-start.4
  533.5 16.0 %collective-permute-start.1 = (bf16[3584,128]{1,0:T(8,128)(2,1)S(1)}, bf16[3584,128]{1,0:T(8,128)(2,1)}, u32[]{:S(2)}, u32[]{:S(2)}) collective-permute-start(bf16[3584,128]{1,0:T(8,128)(2,1)S(1)} %convolution_convert_fusion), channel_id=1, source_target_pairs={{0,32},{32,0},{64,96},{96,64},{128,160},{160,128},{192,224},{224,1... | collective-permute-start | bytes 2752520 | tf_op jit(solution)/shard_map/ppermute | solution.py:12
  540.1 11.7 %collective-permute-start = (bf16[3584,128]{1,0:T(8,128)(2,1)}, bf16[3584,128]{1,0:T(8,128)(2,1)}, u32[]{:S(2)}, u32[]{:S(2)}) collective-permute-start(bf16[3584,128]{1,0:T(8,128)(2,1)} %convolution_convert_fusion.1), channel_id=1, source_target_pairs={{0,32},{32,0},{64,96},{96,64},{128,160},{160,128},{192,224},{224,1... | collective-permute-start | bytes 2752520 | tf_op jit(solution)/shard_map/ppermute | solution.py:12
  547.5 6.9 collective-permute-start.2
where the time goes:
time: 777 us; the launch traced here: 770 us
  waiting for transfers between devices  372 us (48%)
  blocking collectives  212 us (27%)
  local copies, waits for them, and re-layouts  67.9 us (9%)
  matrix products  50.4 us (6%)
  starting transfers between devices  34.9 us (4%)
  other arithmetic  31.8 us (4%)
    all_to_all x1, blocking collectives, shards(): lax.all_to_all(cot_send, 'expert', split_axis=0, concat_axis=0, tiled=True)  212 us
    all_to_all x1, waiting for transfers between devices, shards(): lax.all_to_all(row_grad.reshape(devices_count, capacity, feature_count),...  188 us
    all_to_all x1, waiting for transfers between devices, shards(): lax.all_to_all(row_send, 'expert', split_axis=0, concat_axis=0, tiled=True)  184 us
    dot_general x3, matrix products, contract_rows(): lax.dot_general(left, right, (((0,), (0,)), ((), ())), preferred_element_...  18.8 us
    dot_general x3, matrix products, contract_cols(): lax.dot_general(left, right, (((1,), (1,)), ((), ())), preferred_element_...  15.6 us
  transfers between devices with their start and end apart: 7, of which 2 were waited for; matrix products, arithmetic and copies ran while one was open for 10% of the time, Pallas kernels for 0%

commit v1 on v0

v1 whole, which is shorter than its diff:
```python
import functools

import jax
import jax.numpy as jnp
import numpy as np
from jax import lax
from jax.experimental import pallas as pl
from jax.experimental.pallas import tpu as pltpu
from jax.sharding import PartitionSpec as P

MESH = pl.DeviceIdType.MESH
BF = jnp.bfloat16
F32 = jnp.float32
ROWS = 32
LANES = 128
FOLD = 16
SCALAR_ROW = 28
NY, NZ = 4, 8
GAIN_LIMIT = {(0, 0): 4, (0, 1): 3, (1, 0): 3, (1, 1): 4}


def dot(left, right):
    return jnp.dot(left, right, preferred_element_type=F32)


def dot_tn(left, right):
    return lax.dot_general(left, right, (((0,), (0,)), ((), ())), preferred_element_type=F32)


def dot_nt(left, right):
    return lax.dot_general(left, right, (((1,), (1,)), ((), ())), preferred_element_type=F32)


def fold_matrices(chunks):
    spread = np.zeros((chunks * FOLD, NZ * ROWS), np.float32)
    for chunk in range(chunks):
        for slot in range(NZ):
            spread[chunk * FOLD + slot, slot * ROWS + chunk] = 1.0
    place = np.zeros((NZ * ROWS, NZ * ROWS + FOLD), np.float32)
    for slot in range(NZ):
        place[slot * ROWS + SCALAR_ROW, slot * ROWS : (slot + 1) * ROWS] = 1.0
        place[slot * ROWS + SCALAR_ROW, NZ * ROWS + slot] = 1.0
    return jnp.asarray(spread, BF), jnp.asarray(spread.T, BF), jnp.asarray(place, BF)


def kernel(
    ids_col, ids_row, route, tokens, cot, w_gate, w_up, w_down, spread, spread_t, place,
    token_out, route_out, gu_out, down_out,
    ag, back, ring, stage, ret, acc, other, xq, cq, gu_w, gu_wt, down_wt, ov_rows, ov_grad, ov_hidden, stack, scaled,
    w_sem, y_send, y_recv, ag_send, ag_recv, rs_send, rs_recv, r_send, r_recv, p_send, p_recv,
):
    features = tokens.shape[1]
    chunks = features // LANES
    pairs = chunks // 2
    half = chunks // 2
    main = NZ * ROWS
    me_p = lax.axis_index("pipe")
    me_e = lax.axis_index("expert")
    y = lax.div(me_e, NZ)
    z = lax.rem(me_e, NZ)
    right = (me_p, y * NZ + lax.rem(z + 1, NZ))
    left = (me_p, y * NZ + lax.rem(z + NZ - 1, NZ))
    partner = (me_p + 1 - 2 * lax.rem(me_p, 2), me_e)
    ring_to = (right, left)

    def y_device(apart):
        return (me_p, lax.rem(y + apart, NY) * NZ + z)

    def weight_copies():
        return (
            pltpu.make_async_copy(w_gate, gu_w.at[:, 0:LANES], w_sem.at[0]),
            pltpu.make_async_copy(w_up, gu_w.at[:, LANES : 2 * LANES], w_sem.at[1]),
        )

    for copy in weight_copies():
        copy.start()

    barrier = pltpu.get_barrier_semaphore()
    for device in (right, left, y_device(1), y_device(2), y_device(3), partner):
        pl.semaphore_signal(barrier, inc=1, device_id=device, device_id_type=MESH)

    def y_copy(q, kind):
        return pltpu.make_async_remote_copy(
            src_ref=stage.at[q - 1, kind], dst_ref=ag.at[q, kind, 0],
            send_sem=y_send.at[q, kind], recv_sem=y_recv.at[q, kind],
            device_id=y_device(q), device_id_type=MESH,
        )

    def ag_copy(q, kind, way, hop):
        if way == 0:
            source, target = (NZ - hop + 1) % NZ, NZ - hop
        else:
            source, target = hop - 1, hop
        slot = kind * 2 + way
        return pltpu.make_async_remote_copy(
            src_ref=ag.at[q, kind, source], dst_ref=ag.at[q, kind, target],
            send_sem=ag_send.at[q, slot, hop - 1], recv_sem=ag_recv.at[q, slot, hop - 1],
            device_id=ring_to[way], device_id_type=MESH,
        )

    def part_of(part):
        return pl.ds(0, half) if part == 0 else pl.ds(half, chunks + 1 - half)

    def rs_slot(part, way, hop):
        hops = GAIN_LIMIT[(part, way)]
        return hops - hop if way == 0 else (NZ - hops + hop) % NZ

    def rs_copy(q, part, way, hop):
        slot = part * 2 + way
        extent = half if part == 0 else chunks + 1 - half
        return pltpu.make_async_remote_copy(
            src_ref=back.at[q, rs_slot(part, way, hop - 1), part_of(part)],
            dst_ref=ring.at[q, slot, hop - 1, pl.ds(0, extent)],
            send_sem=rs_send.at[q, slot, hop - 1], recv_sem=rs_recv.at[q, slot, hop - 1],
            device_id=ring_to[way], device_id_type=MESH,
        )

    def ret_copy(q):
        return pltpu.make_async_remote_copy(
            src_ref=back.at[q, 0], dst_ref=ret.at[q],
            send_sem=r_send.at[q], recv_sem=r_recv.at[q],
            device_id=y_device(NY - q), device_id_type=MESH,
        )

    def pair_copies():
        return (
            pltpu.make_async_remote_copy(
                src_ref=gu_out, dst_ref=other.at[0 : 2 * LANES], send_sem=p_send.at[0], recv_sem=p_recv.at[0],
                device_id=partner, device_id_type=MESH,
            ),
            pltpu.make_async_remote_copy(
                src_ref=down_out, dst_ref=other.at[2 * LANES : 3 * LANES], send_sem=p_send.at[1], recv_sem=p_recv.at[1],
                device_id=partner, device_id_type=MESH,
            ),
        )

    def codes():
        shift = y.astype(F32)
        col = ids_col[...].astype(F32) - shift
        col = jnp.where(col < 0, col + NY, col)
        row = ids_row[...].astype(F32) - shift
        row = jnp.where(row < 0, row + NY, row)
        count = col.shape[0]
        first = lax.broadcasted_iota(jnp.int32, (count, count), 0)
        second = lax.broadcasted_iota(jnp.int32, (count, count), 1)
        same = jnp.where(col == row, 1.0, 0.0)
        slot_row = jnp.sum(jnp.where(first < second, same, 0.0), axis=0, keepdims=True)
        slot_col = jnp.sum(jnp.where(second < first, same, 0.0), axis=1, keepdims=True)
        code_row = jnp.where(slot_row < ROWS, row * ROWS + slot_row, NY * ROWS + row)
        code_col = jnp.where(slot_col < ROWS, col * ROWS + slot_col, NY * ROWS + col)
        return col, slot_col, code_row, code_col

    def one_hot(code, shape, dim, start=0):
        places = lax.broadcasted_iota(jnp.int32, shape, dim) + start
        return jnp.where(places.astype(F32) == code, 1.0, 0.0).astype(BF)

    count = tokens.shape[0]
    _, _, code_row, _ = codes()
    pick = one_hot(code_row, (NY * ROWS + FOLD, count), 0)
    scaled[...] = (cot[...].astype(F32) * route[...].astype(F32)).astype(BF)
    for kind, values in ((0, tokens), (1, scaled)):
        for pair in range(pairs):
            rows = dot(pick, values[:, 2 * LANES * pair : 2 * LANES * (pair + 1)]).astype(BF)
            for side in range(2):
                chunk = 2 * pair + side
                part = rows[:, side * LANES : (side + 1) * LANES]
                ag[0, kind, 0, chunk] = part[0:ROWS]
                for q in range(1, NY):
                    stage[q - 1, kind, chunk] = part[q * ROWS : (q + 1) * ROWS]
                stack[chunk * FOLD : (chunk + 1) * FOLD] = part[NY * ROWS : NY * ROWS + FOLD]
        folded = dot(spread_t[0 : NY * ROWS], stack[...]).astype(BF)
        ag[0, kind, 0, chunks] = folded[0:ROWS]
        for q in range(1, NY):
            stage[q - 1, kind, chunks] = folded[q * ROWS : (q + 1) * ROWS]
        if kind == 0:
            pl.semaphore_wait(barrier, 6)
        for way in range(2):
            ag_copy(0, kind, way, 1).start()
        for q in range(1, NY):
            y_copy(q, kind).start()

    for copy in weight_copies():
        copy.wait()
    for chunk in range(chunks):
        span = slice(chunk * LANES, (chunk + 1) * LANES)
        gu_wt[:, span] = gu_w[span, :].T
        down_wt[span, :] = w_down[:, span].T
    acc[...] = jnp.zeros_like(acc)

    def gather_hop(q, hop):
        for kind in range(2):
            for way in range(2):
                if hop <= GAIN_LIMIT[(kind, way)]:
                    ag_copy(q, kind, way, hop).wait_recv()
                    if hop < GAIN_LIMIT[(kind, way)]:
                        ag_copy(q, kind, way, hop + 1).start()

    def reduce_start(q):
        for part in range(2):
            for way in range(2):
                rs_copy(q, part, way, 1).start()

    def reduce_hop(q, hop):
        for part in range(2):
            for way in range(2):
                hops = GAIN_LIMIT[(part, way)]
                if hop <= hops:
                    extent = half if part == 0 else chunks + 1 - half
                    rs_copy(q, part, way, hop).wait_recv()
                    target = back.at[q, rs_slot(part, way, hop), part_of(part)]
                    came = ring[q, part * 2 + way, hop - 1, 0:extent]
                    target[...] = (target[...].astype(F32) + came.astype(F32)).astype(BF)
                    if hop < hops:
                        rs_copy(q, part, way, hop + 1).start()

    def compute_rows(q):
        for kind, rows in ((0, xq), (1, cq)):
            folded = ag[q, kind, :, chunks].reshape(main, LANES)
            unfolded = dot(spread[...], folded).astype(BF)
            for chunk in range(chunks):
                span = slice(chunk * LANES, (chunk + 1) * LANES)
                rows[0:main, span] = ag[q, kind, :, chunk].reshape(main, LANES)
                extra = unfolded[chunk * FOLD : (chunk + 1) * FOLD]
                rows[main : main + FOLD, span] = extra
                ov_rows[kind, pl.ds(pl.multiple_of(q * FOLD, FOLD), FOLD), span] = extra
        pre = dot(xq[...], gu_w[...])
        gate, up = pre[:, 0:LANES], pre[:, LANES : 2 * LANES]
        hidden_grad = dot(cq[...], down_wt[...])
        sig = jax.nn.sigmoid(gate)
        hidden = (gate * sig * up).astype(BF)
        grad_gate = (hidden_grad * up * sig * (1.0 + gate * (1.0 - sig))).astype(BF)
        grad_up = (hidden_grad * gate * sig).astype(BF)
        grads = jnp.concatenate([grad_gate, grad_up], axis=1)
        mine = pl.ds(pl.multiple_of(q * FOLD, FOLD), FOLD)
        ov_grad[mine] = grads[main : main + FOLD]
        ov_hidden[mine] = hidden[main : main + FOLD]
        for pair in range(pairs):
            rows = dot(grads, gu_wt[:, 2 * LANES * pair : 2 * LANES * (pair + 1)]).astype(BF)
            for side in range(2):
                chunk = 2 * pair + side
                part = rows[:, side * LANES : (side + 1) * LANES]
                back[q, :, chunk] = part[0:main].reshape(NZ, ROWS, LANES)
                stack[chunk * FOLD : (chunk + 1) * FOLD] = part[main : main + FOLD]
        slot = jnp.sum(hidden.astype(F32) * hidden_grad, axis=1, keepdims=True)
        which = lax.broadcasted_iota(jnp.int32, (main + FOLD, LANES), 0)
        lane = lax.broadcasted_iota(jnp.int32, (main + FOLD, LANES), 1)
        wanted = jnp.where(which < main, lax.rem(which, ROWS), ROWS)
        spots = jnp.where(lane == wanted, slot, 0.0).astype(BF)
        folded = dot(spread_t[...], stack[...]) + dot(place[...], spots)
        back[q, :, chunks] = folded.astype(BF).reshape(NZ, ROWS, LANES)
        return grads[0:main], hidden[0:main]

    def compute_weights(grads, hidden):
        width = 4 * LANES
        for start in range(0, features, width):
            span = slice(start, start + width)
            acc[0 : 2 * LANES, span] += dot_tn(grads, xq[0:main, span])
            acc[2 * LANES : 3 * LANES, span] += dot_tn(hidden, cq[0:main, span])

    def next_quarter(q):
        for kind in range(2):
            y_copy(q, kind).wait_recv()
            for way in range(2):
                ag_copy(q, kind, way, 1).start()

    def finish_return(q):
        @pl.when(q > 0)
        def _():
            ret_copy(q).start()

    def quarter(q, carry):
        @pl.when(q == 0)
        def _():
            for hop in range(1, 5):
                gather_hop(q, hop)

        @pl.when(q > 0)
        def _():
            for hop in range(1, 5):
                gather_hop(q, hop)
                reduce_hop(q - 1, hop)
            finish_return(q - 1)

        @pl.when(q < NY - 1)
        def _():
            next_quarter(q + 1)

        grads, hidden = compute_rows(q)
        reduce_start(q)
        compute_weights(grads, hidden)
        return carry

    lax.fori_loop(0, NY, quarter, 0)

    width = 4 * LANES
    for start in range(0, features, width):
        span = slice(start, start + width)
        acc[0 : 2 * LANES, span] += dot_tn(ov_grad[...], ov_rows[0, :, span])
        acc[2 * LANES : 3 * LANES, span] += dot_tn(ov_hidden[...], ov_rows[1, :, span])
        gu_out[:, span] = acc[0 : 2 * LANES, span].astype(BF)
        down_out[:, span] = acc[2 * LANES : 3 * LANES, span].astype(BF)
    for copy in pair_copies():
        copy.start()

    for hop in range(1, 5):
        reduce_hop(NY - 1, hop)
    ret_copy(NY - 1).start()
    ret[0] = back[0, 0]

    for copy in pair_copies():
        copy.wait()
    for start in range(0, features, width):
        span = slice(start, start + width)
        gu_out[:, span] = (acc[0 : 2 * LANES, span] + other[0 : 2 * LANES, span].astype(F32)).astype(BF)
        down_out[:, span] = (acc[2 * LANES : 3 * LANES, span] + other[2 * LANES : 3 * LANES, span].astype(F32)).astype(BF)

    for q in range(1, NY):
        ret_copy(q).wait_recv()

    col, slot_col, _, code_col = codes()
    unpick = one_hot(code_col, (count, NY * ROWS), 1)
    unpick_fold = one_hot(code_col, (count, FOLD), 1, NY * ROWS)
    folded = ret[:, chunks].reshape(NY * ROWS, LANES)
    unfolded = dot(spread[:, 0 : NY * ROWS], folded).astype(BF)
    for chunk in range(chunks):
        rows = ret[:, chunk].reshape(NY * ROWS, LANES)
        total = dot(unpick, rows) + dot(unpick_fold, unfolded[chunk * FOLD : (chunk + 1) * FOLD])
        token_out[:, chunk * LANES : (chunk + 1) * LANES] = total.astype(BF)
    lane = lax.broadcasted_iota(jnp.int32, (count, LANES), 1).astype(F32)
    total = jnp.zeros((count, LANES), F32)
    for q in range(NY):
        entry = ret[q, chunks].astype(F32)[SCALAR_ROW : SCALAR_ROW + 1]
        total = total + jnp.where((lane == slot_col) & (col == q), entry, 0.0)
    slot_sum = jnp.sum(total, axis=1, keepdims=True)
    route_out[...] = (slot_sum / route[...].astype(F32)).astype(BF)

    for q in range(NY):
        for kind in range(2):
            if q > 0:
                y_copy(q, kind).wait_send()
            for way in range(2):
                for hop in range(1, GAIN_LIMIT[(kind, way)] + 1):
                    ag_copy(q, kind, way, hop).wait_send()
                    rs_copy(q, kind, way, hop).wait_send()
        if q > 0:
            ret_copy(q).wait_send()


def shards(tokens, expert_ids, route_weight, cotangent, w_gate, w_up, w_down):
    count, features = tokens.shape[1:]
    hidden = w_gate.shape[2]
    chunks = features // LANES
    spread, spread_t, place = fold_matrices(chunks)
    vmem = pl.BlockSpec(memory_space=pltpu.VMEM)
    anywhere = pl.BlockSpec(memory_space=pl.ANY)
    message = (chunks + 1, ROWS, LANES)
    larger = chunks + 1 - chunks // 2
    token_grad, route_grad, gu_grad, down_grad = pl.pallas_call(
        kernel,
        out_shape=(
            jax.ShapeDtypeStruct((count, features), BF),
            jax.ShapeDtypeStruct((count, 1), BF),
            jax.ShapeDtypeStruct((2 * hidden, features), BF),
            jax.ShapeDtypeStruct((hidden, features), BF),
        ),
        in_specs=[vmem] * 5 + [anywhere] * 2 + [vmem] * 4,
        out_specs=(vmem, vmem, vmem, vmem),
        scratch_shapes=[
            pltpu.VMEM((NY, 2, NZ) + message, BF),
            pltpu.VMEM((NY, NZ) + message, BF),
            pltpu.VMEM((NY, 4, 4, larger, ROWS, LANES), BF),
            pltpu.VMEM((NY - 1, 2) + message, BF),
            pltpu.VMEM((NY,) + message, BF),
            pltpu.VMEM((3 * hidden, features), F32),
            pltpu.VMEM((3 * hidden, features), BF),
            pltpu.VMEM((NZ * ROWS + FOLD, features), BF),
            pltpu.VMEM((NZ * ROWS + FOLD, features), BF),
            pltpu.VMEM((features, 2 * hidden), BF),
            pltpu.VMEM((2 * hidden, features), BF),
            pltpu.VMEM((features, hidden), BF),
            pltpu.VMEM((2, NY * FOLD, features), BF),
            pltpu.VMEM((NY * FOLD, 2 * hidden), BF),
            pltpu.VMEM((NY * FOLD, hidden), BF),
            pltpu.VMEM((chunks * FOLD, LANES), BF),
            pltpu.VMEM((count, features), BF),
            pltpu.SemaphoreType.DMA((2,)),
            pltpu.SemaphoreType.DMA((NY, 2)),
            pltpu.SemaphoreType.DMA((NY, 2)),
            pltpu.SemaphoreType.DMA((NY, 4, 4)),
            pltpu.SemaphoreType.DMA((NY, 4, 4)),
            pltpu.SemaphoreType.DMA((NY, 4, 4)),
            pltpu.SemaphoreType.DMA((NY, 4, 4)),
            pltpu.SemaphoreType.DMA((NY,)),
            pltpu.SemaphoreType.DMA((NY,)),
            pltpu.SemaphoreType.DMA((2,)),
            pltpu.SemaphoreType.DMA((2,)),
        ],
        compiler_params=pltpu.CompilerParams(
            collective_id=0, has_side_effects=True, vmem_limit_bytes=63 * 1024 * 1024
        ),
        cost_estimate=pl.CostEstimate(flops=8_000_000_000, bytes_accessed=10_000_000, transcendentals=140_000),
    )(
        expert_ids[0], expert_ids[0].reshape(1, count), route_weight[0], tokens[0], cotangent[0],
        w_gate[0], w_up[0], w_down[0], spread, spread_t, place,
    )
    grad_gate = gu_grad[0:hidden].T
    grad_up = gu_grad[hidden : 2 * hidden].T
    return (token_grad[None], route_grad[None], grad_gate[None], grad_up[None], down_grad[None])


def solution(mesh):
    rows = P("pipe", "expert", None)
    columns = P("pipe", None, "expert")
    return jax.shard_map(
        shards, mesh=mesh,
        in_specs=(rows, rows, rows, rows, columns, columns, rows),
        out_specs=(rows, rows, columns, columns, rows),
        check_vma=False,
    )
```

time: 777 us -> 256 us (0.33)
  waiting for transfers between devices: 372 us -> 0 us
  Pallas kernels: 0 us -> 245 us
  blocking collectives: 212 us -> 0 us
  local copies, waits for them, and re-layouts: 67.9 us -> 8.74 us
  matrix products: 50.4 us -> 0 us
  starting transfers between devices: 34.9 us -> 0 us
  other arithmetic: 31.8 us -> 1.39 us
    all_to_all x4 -> x0, waiting for transfers between devices: 372 us -> none  [the longest x1 188 us: shards(): lax.all_to_all(row_grad.reshape(devices_count, capacity, feature_count),...]
    pallas_call x0 -> x1, Pallas kernels: none -> 245 us  [shards(): pl.pallas_call(kernel, out_shape=(jax.ShapeDtypeStruct((count, features),...]
    all_to_all x1 -> x0, blocking collectives: 212 us -> none  [shards(): lax.all_to_all(cot_send, 'expert', split_axis=0, concat_axis=0, tiled=True)]
    dot_general x9 -> x0, matrix products: 50.4 us -> none  [the longest x3 18.8 us: contract_rows(): lax.dot_general(left, right, (((0,), (0,)), ((), ())), preferred_element_...]
    all_to_all x4 -> x0, starting transfers between devices: 34 us -> none  [the longest x1 11.4 us: shards(): lax.all_to_all(weight_send, 'expert', split_axis=0, concat_axis=0, tiled=...]
    reshape x5 -> x0, local copies, waits for them, and re-layouts: 24.9 us -> none  [the longest x1 8.97 us: shards(): grouped = back_rows.reshape(EXPERTS, group_size, capacity, feature_count)]
    convert_element_type x4 -> x0, local copies, waits for them, and re-layouts: 19 us -> none  [the longest x1 10.2 us: expert_backward(): cot_wide = cot_rows.astype(jnp.float32)]
    gather x7 -> x0, local copies, waits for them, and re-layouts: 17.3 us -> none  [the longest x4 7.13 us: pack_rows(): picked = values[jnp.maximum(source_row, 0) // top_count]]
  transfers between devices with their start and end apart: 7 -> 0, of which waited for: 2 -> 0; matrix products, arithmetic and copies ran while one was open for 10% -> 0% of each run, Pallas kernels for 0% -> 0%
where the time goes in v1:
time: 256 us
  Pallas kernels  245 us (96%)
  local copies, waits for them, and re-layouts  8.74 us (3%)
    pallas_call x1, Pallas kernels, shards(): pl.pallas_call(kernel, out_shape=(jax.ShapeDtypeStruct((count, features),...  245 us

profile of v1, /device:TPU:32, one launch (start us, length us, event | category | flops | bytes accessed | tf_op | source)
XLA Modules:
  0.0 255.6 jit_solution(1363741999614499940)
XLA Ops:
  0.6 1.4 copy.20.route
  2.0 1.4 copy.19.ids_col
  3.4 244.8 %shard_map.137 = (bf16[128,3584]{1,0:T(8,128)(2,1)}, bf16[128,1]{1,0:T(8,128)(2,1)}, bf16[256,3584]{1,0:T(8,128)(2,1)}, bf16[128,3584]{1,0:T(8,128)(2,1)}) custom-call(s32[128,1]{1,0:T(8,128)} %copy.19.ids_col, s32[1,128]{1,0:T(1,128)} %bitcast.23, bf16[128,1]{1,0:T(8,128)(2,1)} %copy.20.route, bf16[128,3584]{1,0:T(8,128)(2,1)} %bitcast.25, ...), custom_call_target="tpu_custom_call" | custom-call | flops 8000000000 | bytes 10000000 | tf_op jit(solution)/shard_map/pallas_call | solution.py:358
  248.2 1.4 reduce
  249.6 1.6 slice_bitcast_fusion
  251.2 0.0 copy-start.1
  251.2 1.3 copy.22
  252.5 0.0 copy-start
  252.5 1.3 copy.21
  253.8 0.0 copy-done.1
  253.8 0.9 copy.25
  254.7 0.0 copy-done
  254.7 0.9 copy.26
Async XLA Ops:
  251.2 2.6 copy-start.1
  252.5 2.2 copy-start

commit v2 on v1

--- a/solution.py
+++ b/solution.py
@@ -1,5 +1,3 @@
-import functools
-
 import jax
 import jax.numpy as jnp
 import numpy as np
@@ -14,9 +12,9 @@
 ROWS = 32
 LANES = 128
 FOLD = 16
-SCALAR_ROW = 28
+HIGH, LOW = 28, 29
 NY, NZ = 4, 8
-GAIN_LIMIT = {(0, 0): 4, (0, 1): 3, (1, 0): 3, (1, 1): 4}
+HOPS = {(0, 0): 4, (0, 1): 3, (1, 0): 3, (1, 1): 4}
 
 
 def dot(left, right):
@@ -36,20 +34,24 @@
     for chunk in range(chunks):
         for slot in range(NZ):
             spread[chunk * FOLD + slot, slot * ROWS + chunk] = 1.0
-    place = np.zeros((NZ * ROWS, NZ * ROWS + FOLD), np.float32)
-    for slot in range(NZ):
-        place[slot * ROWS + SCALAR_ROW, slot * ROWS : (slot + 1) * ROWS] = 1.0
-        place[slot * ROWS + SCALAR_ROW, NZ * ROWS + slot] = 1.0
+    place = np.zeros((2, NZ * ROWS, NZ * ROWS + FOLD), np.float32)
+    for part, row in ((0, HIGH), (1, LOW)):
+        for slot in range(NZ):
+            place[part, slot * ROWS + row, slot * ROWS : (slot + 1) * ROWS] = 1.0
+            place[part, slot * ROWS + row, NZ * ROWS + slot] = 1.0
     return jnp.asarray(spread, BF), jnp.asarray(spread.T, BF), jnp.asarray(place, BF)
 
 
 def kernel(
-    ids_col, ids_row, route, tokens, cot, w_gate, w_up, w_down, spread, spread_t, place,
-    token_out, route_out, gu_out, down_out,
-    ag, back, ring, stage, ret, acc, other, xq, cq, gu_w, gu_wt, down_wt, ov_rows, ov_grad, ov_hidden, stack, scaled,
+    ids_row, route_row, tokens_in, cot_in, w_gate, w_up, w_down_in, spread, spread_t, place,
+    token_out, route_out, gate_out, up_out, down_out,
+    ag, back, ring, stage, ret, acc, other, xq, cq, gu_w, gu_wt, down_wt, ov_rows, ov_grad, ov_hidden, stack,
     w_sem, y_send, y_recv, ag_send, ag_recv, rs_send, rs_recv, r_send, r_recv, p_send, p_recv,
 ):
-    features = tokens.shape[1]
+    count, features = tokens_in.shape
+    tokens, cot, w_down = xq.at[0:count], xq.at[count : 2 * count], cq.at[0:count]
+    own_gu = gu_wt
+    scaled = cq.at[count : 2 * count]
     chunks = features // LANES
     pairs = chunks // 2
     half = chunks // 2
@@ -70,9 +72,14 @@
         return (
             pltpu.make_async_copy(w_gate, gu_w.at[:, 0:LANES], w_sem.at[0]),
             pltpu.make_async_copy(w_up, gu_w.at[:, LANES : 2 * LANES], w_sem.at[1]),
-        )
-
-    for copy in weight_copies():
+            pltpu.make_async_copy(w_down_in, w_down, w_sem.at[2]),
+        )
+
+    loads = (
+        pltpu.make_async_copy(tokens_in, tokens, w_sem.at[3]),
+        pltpu.make_async_copy(cot_in, cot, w_sem.at[4]),
+    )
+    for copy in loads + weight_copies():
         copy.start()
 
     barrier = pltpu.get_barrier_semaphore()
@@ -102,7 +109,7 @@
         return pl.ds(0, half) if part == 0 else pl.ds(half, chunks + 1 - half)
 
     def rs_slot(part, way, hop):
-        hops = GAIN_LIMIT[(part, way)]
+        hops = HOPS[(part, way)]
         return hops - hop if way == 0 else (NZ - hops + hop) % NZ
 
     def rs_copy(q, part, way, hop):
@@ -125,7 +132,7 @@
     def pair_copies():
         return (
             pltpu.make_async_remote_copy(
-                src_ref=gu_out, dst_ref=other.at[0 : 2 * LANES], send_sem=p_send.at[0], recv_sem=p_recv.at[0],
+                src_ref=own_gu, dst_ref=other.at[0 : 2 * LANES], send_sem=p_send.at[0], recv_sem=p_recv.at[0],
                 device_id=partner, device_id_type=MESH,
             ),
             pltpu.make_async_remote_copy(
@@ -134,13 +141,15 @@
             ),
         )
 
+    def to_column(row):
+        first = lax.broadcasted_iota(jnp.int32, (count, count), 0)
+        second = lax.broadcasted_iota(jnp.int32, (count, count), 1)
+        return jnp.sum(jnp.where(first == second, row, 0.0), axis=1, keepdims=True)
+
     def codes():
-        shift = y.astype(F32)
-        col = ids_col[...].astype(F32) - shift
-        col = jnp.where(col < 0, col + NY, col)
-        row = ids_row[...].astype(F32) - shift
-        row = jnp.where(row < 0, row + NY, row)
-        count = col.shape[0]
+        rel = ids_row[...].astype(F32) - y.astype(F32)
+        row = jnp.where(rel < 0, rel + NY, rel)
+        col = to_column(row)
         first = lax.broadcasted_iota(jnp.int32, (count, count), 0)
         second = lax.broadcasted_iota(jnp.int32, (count, count), 1)
         same = jnp.where(col == row, 1.0, 0.0)
@@ -154,11 +163,13 @@
         places = lax.broadcasted_iota(jnp.int32, shape, dim) + start
         return jnp.where(places.astype(F32) == code, 1.0, 0.0).astype(BF)
 
-    count = tokens.shape[0]
     _, _, code_row, _ = codes()
     pick = one_hot(code_row, (NY * ROWS + FOLD, count), 0)
-    scaled[...] = (cot[...].astype(F32) * route[...].astype(F32)).astype(BF)
+    loads[0].wait()
     for kind, values in ((0, tokens), (1, scaled)):
+        if kind == 1:
+            loads[1].wait()
+            scaled[...] = (cot[...].astype(F32) * to_column(route_row[...].astype(F32))).astype(BF)
         for pair in range(pairs):
             rows = dot(pick, values[:, 2 * LANES * pair : 2 * LANES * (pair + 1)]).astype(BF)
             for side in range(2):
@@ -190,9 +201,9 @@
     def gather_hop(q, hop):
         for kind in range(2):
             for way in range(2):
-                if hop <= GAIN_LIMIT[(kind, way)]:
+                if hop <= HOPS[(kind, way)]:
                     ag_copy(q, kind, way, hop).wait_recv()
-                    if hop < GAIN_LIMIT[(kind, way)]:
+                    if hop < HOPS[(kind, way)]:
                         ag_copy(q, kind, way, hop + 1).start()
 
     def reduce_start(q):
@@ -200,16 +211,24 @@
             for way in range(2):
                 rs_copy(q, part, way, 1).start()
 
+    def merge(first, second):
+        total = first.astype(F32) + second.astype(F32)
+        sums = total[HIGH : HIGH + 1] + total[LOW : LOW + 1]
+        high = sums.astype(BF).astype(F32)
+        row = lax.broadcasted_iota(jnp.int32, (ROWS, LANES), 0)
+        return jnp.where(row == HIGH, high, jnp.where(row == LOW, sums - high, total)).astype(BF)
+
     def reduce_hop(q, hop):
         for part in range(2):
             for way in range(2):
-                hops = GAIN_LIMIT[(part, way)]
+                hops = HOPS[(part, way)]
                 if hop <= hops:
-                    extent = half if part == 0 else chunks + 1 - half
                     rs_copy(q, part, way, hop).wait_recv()
                     target = back.at[q, rs_slot(part, way, hop), part_of(part)]
-                    came = ring[q, part * 2 + way, hop - 1, 0:extent]
-                    target[...] = (target[...].astype(F32) + came.astype(F32)).astype(BF)
+                    came = ring.at[q, part * 2 + way, hop - 1]
+                    target[0:half] = (target[0:half].astype(F32) + came[0:half].astype(F32)).astype(BF)
+                    if part == 1:
+                        target[half] = merge(target[half], came[half])
                     if hop < hops:
                         rs_copy(q, part, way, hop + 1).start()
 
@@ -245,8 +264,10 @@
         which = lax.broadcasted_iota(jnp.int32, (main + FOLD, LANES), 0)
         lane = lax.broadcasted_iota(jnp.int32, (main + FOLD, LANES), 1)
         wanted = jnp.where(which < main, lax.rem(which, ROWS), ROWS)
-        spots = jnp.where(lane == wanted, slot, 0.0).astype(BF)
-        folded = dot(spread_t[...], stack[...]) + dot(place[...], spots)
+        spots = jnp.where(lane == wanted, slot, 0.0)
+        high = spots.astype(BF)
+        low = (spots - high.astype(F32)).astype(BF)
+        folded = dot(spread_t[...], stack[...]) + dot(place[0], high) + dot(place[1], low)
         back[q, :, chunks] = folded.astype(BF).reshape(NZ, ROWS, LANES)
         return grads[0:main], hidden[0:main]
 
@@ -263,55 +284,82 @@
             for way in range(2):
                 ag_copy(q, kind, way, 1).start()
 
-    def finish_return(q):
-        @pl.when(q > 0)
-        def _():
-            ret_copy(q).start()
-
     def quarter(q, carry):
-        @pl.when(q == 0)
-        def _():
-            for hop in range(1, 5):
-                gather_hop(q, hop)
-
-        @pl.when(q > 0)
-        def _():
-            for hop in range(1, 5):
-                gather_hop(q, hop)
-                reduce_hop(q - 1, hop)
-            finish_return(q - 1)
+        gather_hop(q, 3)
+
+        @pl.when(q >= 2)
+        def _():
+            reduce_hop(q - 1, 1)
+
+        gather_hop(q, 4)
+
+        @pl.when(q >= 2)
+        def _():
+            reduce_hop(q - 1, 2)
 
         @pl.when(q < NY - 1)
         def _():
-            next_quarter(q + 1)
+            gather_hop(q + 1, 1)
 
         grads, hidden = compute_rows(q)
         reduce_start(q)
+
+        @pl.when(q < NY - 2)
+        def _():
+            next_quarter(q + 2)
+
+        @pl.when(q == 2)
+        def _():
+            reduce_hop(q - 1, 3)
+
+        @pl.when(q < NY - 1)
+        def _():
+            gather_hop(q + 1, 2)
+
+        @pl.when(q == 2)
+        def _():
+            reduce_hop(q - 1, 4)
+            ret_copy(q - 1).start()
+
         compute_weights(grads, hidden)
         return carry
 
+    gather_hop(0, 1)
+    next_quarter(1)
+    gather_hop(0, 2)
     lax.fori_loop(0, NY, quarter, 0)
+    reduce_hop(2, 3)
 
     width = 4 * LANES
     for start in range(0, features, width):
         span = slice(start, start + width)
         acc[0 : 2 * LANES, span] += dot_tn(ov_grad[...], ov_rows[0, :, span])
         acc[2 * LANES : 3 * LANES, span] += dot_tn(ov_hidden[...], ov_rows[1, :, span])
-        gu_out[:, span] = acc[0 : 2 * LANES, span].astype(BF)
+        own_gu[:, span] = acc[0 : 2 * LANES, span].astype(BF)
         down_out[:, span] = acc[2 * LANES : 3 * LANES, span].astype(BF)
     for copy in pair_copies():
         copy.start()
 
-    for hop in range(1, 5):
-        reduce_hop(NY - 1, hop)
-    ret_copy(NY - 1).start()
+    reduce_hop(3, 1)
+    reduce_hop(0, 1)
+    reduce_hop(2, 4)
+    ret_copy(2).start()
+    for hop in range(2, 5):
+        reduce_hop(3, hop)
+        if hop == 4:
+            ret_copy(3).start()
+        reduce_hop(0, hop)
     ret[0] = back[0, 0]
 
     for copy in pair_copies():
         copy.wait()
     for start in range(0, features, width):
         span = slice(start, start + width)
-        gu_out[:, span] = (acc[0 : 2 * LANES, span] + other[0 : 2 * LANES, span].astype(F32)).astype(BF)
+        both = (acc[0 : 2 * LANES, span] + other[0 : 2 * LANES, span].astype(F32)).astype(BF)
+        for part in range(0, width, LANES):
+            here = slice(start + part, start + part + LANES)
+            gate_out[here] = both[0:LANES, part : part + LANES].T
+            up_out[here] = both[LANES : 2 * LANES, part : part + LANES].T
         down_out[:, span] = (acc[2 * LANES : 3 * LANES, span] + other[2 * LANES : 3 * LANES, span].astype(F32)).astype(BF)
 
     for q in range(1, NY):
@@ -329,17 +377,21 @@
     lane = lax.broadcasted_iota(jnp.int32, (count, LANES), 1).astype(F32)
     total = jnp.zeros((count, LANES), F32)
     for q in range(NY):
-        entry = ret[q, chunks].astype(F32)[SCALAR_ROW : SCALAR_ROW + 1]
+        last = ret[q, chunks].astype(F32)
+        entry = last[HIGH : HIGH + 1] + last[LOW : LOW + 1]
         total = total + jnp.where((lane == slot_col) & (col == q), entry, 0.0)
     slot_sum = jnp.sum(total, axis=1, keepdims=True)
-    route_out[...] = (slot_sum / route[...].astype(F32)).astype(BF)
+    first = lax.broadcasted_iota(jnp.int32, (count, count), 0)
+    second = lax.broadcasted_iota(jnp.int32, (count, count), 1)
+    sum_row = jnp.sum(jnp.where(first == second, slot_sum, 0.0), axis=0, keepdims=True)
+    route_out[...] = (sum_row / route_row[...].astype(F32)).astype(BF)
 
     for q in range(NY):
         for kind in range(2):
             if q > 0:
                 y_copy(q, kind).wait_send()
             for way in range(2):
-                for hop in range(1, GAIN_LIMIT[(kind, way)] + 1):
+                for hop in range(1, HOPS[(kind, way)] + 1):
                     ag_copy(q, kind, way, hop).wait_send()
                     rs_copy(q, kind, way, hop).wait_send()
         if q > 0:
@@ -355,16 +407,17 @@
     anywhere = pl.BlockSpec(memory_space=pl.ANY)
     message = (chunks + 1, ROWS, LANES)
     larger = chunks + 1 - chunks // 2
-    token_grad, route_grad, gu_grad, down_grad = pl.pallas_call(
+    token_grad, route_grad, gate_grad, up_grad, down_grad = pl.pallas_call(
         kernel,
         out_shape=(
             jax.ShapeDtypeStruct((count, features), BF),
-            jax.ShapeDtypeStruct((count, 1), BF),
-            jax.ShapeDtypeStruct((2 * hidden, features), BF),
+            jax.ShapeDtypeStruct((1, count), BF),
+            jax.ShapeDtypeStruct((features, hidden), BF),
+            jax.ShapeDtypeStruct((features, hidden), BF),
             jax.ShapeDtypeStruct((hidden, features), BF),
         ),
-        in_specs=[vmem] * 5 + [anywhere] * 2 + [vmem] * 4,
-        out_specs=(vmem, vmem, vmem, vmem),
+        in_specs=[vmem] * 2 + [anywhere] * 5 + [vmem] * 3,
+        out_specs=(vmem,) * 5,
         scratch_shapes=[
             pltpu.VMEM((NY, 2, NZ) + message, BF),
             pltpu.VMEM((NY, NZ) + message, BF),
@@ -382,8 +435,7 @@
             pltpu.VMEM((NY * FOLD, 2 * hidden), BF),
             pltpu.VMEM((NY * FOLD, hidden), BF),
             pltpu.VMEM((chunks * FOLD, LANES), BF),
-            pltpu.VMEM((count, features), BF),
-            pltpu.SemaphoreType.DMA((2,)),
+            pltpu.SemaphoreType.DMA((5,)),
             pltpu.SemaphoreType.DMA((NY, 2)),
             pltpu.SemaphoreType.DMA((NY, 2)),
             pltpu.SemaphoreType.DMA((NY, 4, 4)),
@@ -400,12 +452,10 @@
         ),
         cost_estimate=pl.CostEstimate(flops=8_000_000_000, bytes_accessed=10_000_000, transcendentals=140_000),
     )(
-        expert_ids[0], expert_ids[0].reshape(1, count), route_weight[0], tokens[0], cotangent[0],
+        expert_ids.reshape(1, count), route_weight.reshape(1, count), tokens[0], cotangent[0],
         w_gate[0], w_up[0], w_down[0], spread, spread_t, place,
     )
-    grad_gate = gu_grad[0:hidden].T
-    grad_up = gu_grad[hidden : 2 * hidden].T
-    return (token_grad[None], route_grad[None], grad_gate[None], grad_up[None], down_grad[None])
+    return (token_grad[None], route_grad.reshape(1, count, 1), gate_grad[None], up_grad[None], down_grad[None])
 
 
 def solution(mesh):

time: 256 us -> 247 us (0.965)
  Pallas kernels: 245 us -> 239 us
    pallas_call x1, Pallas kernels: 245 us -> 239 us  [shards(): pl.pallas_call(kernel, out_shape=(jax.ShapeDtypeStruct((count, features),...]
    squeeze x2 -> x0, local copies, waits for them, and re-layouts: 2.77 us -> none  [the longest x1 1.39 us: shards(): expert_ids[0]]
    unnamed x8 -> x13, local copies, waits for them, and re-layouts: 4.39 us -> 6.7 us
where the time goes in v2:
time: 247 us; the launch traced here: 246 us
  Pallas kernels  239 us (97%)
  local copies, waits for them, and re-layouts  6.7 us (3%)
    pallas_call x1, Pallas kernels, shards(): pl.pallas_call(kernel, out_shape=(jax.ShapeDtypeStruct((count, features),...  239 us
    unnamed x13, local copies, waits for them, and re-layouts  6.7 us

profile of v2, /device:TPU:32, one launch (start us, length us, event | category | flops | bytes accessed | tf_op | source)
XLA Modules:
  0.0 245.9 jit_solution(8154612192965178553)
XLA Ops:
  0.6 238.6 %shard_map.137 = (bf16[128,3584]{1,0:T(8,128)(2,1)}, bf16[1,128]{1,0:T(2,128)(2,1)}, bf16[3584,128]{1,0:T(8,128)(2,1)}, bf16[3584,128]{1,0:T(8,128)(2,1)}, bf16[128,3584]{1,0:T(8,128)(2,1)}) custom-call(s32[1,128]{1,0:T(1,128)} %bitcast.21, bf16[1,128]{1,0:T(2,128)(2,1)} %bitcast.22, bf16[128,3584]{1,0:T(8,128)(2,1)} %bitcast.16, ...), custom_call_target="tpu_custom_call" | custom-call | flops 8000000000 | bytes 10000000 | tf_op jit(solution)/shard_map/pallas_call | solution.py:410
  239.2 0.0 copy-start.3
  239.2 0.0 copy-start.2
  239.2 2.2 copy.20
  241.5 0.0 copy-done.3
  241.5 0.5 copy.21
  242.0 0.0 copy-done.2
  242.0 0.0 copy-start.1
  242.0 0.9 copy.22
  242.9 0.6 copy-done.1
  243.5 0.0 copy-start
  243.5 0.9 copy.23
  244.4 0.6 copy-done
  245.0 0.9 copy.24
Async XLA Ops:
  239.2 2.3 copy-start.3
  239.2 2.8 %copy-start.2 = (bf16[3584,128]{1,0:T(8,128)(2,1)S(1)}, bf16[3584,128]{1,0:T(8,128)(2,1)}, u32[]{:S(2)}) copy-start(bf16[3584,128]{1,0:T(8,128)(2,1)} %get-tuple-element.12) | copy-start | bytes 2752516
  242.0 1.5 copy-start.1
  243.5 1.5 copy-start

commit v3 on v0

v3 whole, which is shorter than its diff:
```python
import jax
import jax.numpy as jnp
import numpy as np
from jax import lax
from jax.experimental import pallas as pl
from jax.experimental.pallas import tpu as pltpu
from jax.sharding import PartitionSpec as P

MESH = pl.DeviceIdType.MESH
BF = jnp.bfloat16
F32 = jnp.float32
ROWS = 32
LANES = 128
FOLD = 16
HIGH, LOW = 28, 29
NY, NZ, LINE = 4, 8, 4
MAIN = LINE * ROWS
QROWS = MAIN + FOLD


def dot(left, right):
    return jnp.dot(left, right, preferred_element_type=F32)


def fold_matrices(chunks):
    spread = np.zeros((chunks * FOLD, MAIN), np.float32)
    for chunk in range(chunks):
        for slot in range(LINE):
            spread[chunk * FOLD + slot, slot * ROWS + chunk] = 1.0
    place = np.zeros((2, MAIN, QROWS), np.float32)
    for part, row in ((0, HIGH), (1, LOW)):
        for slot in range(LINE):
            place[part, slot * ROWS + row, slot * ROWS : (slot + 1) * ROWS] = 1.0
            place[part, slot * ROWS + row, MAIN + slot] = 1.0
    return jnp.asarray(spread, BF), jnp.asarray(spread.T, BF), jnp.asarray(place, BF)


def kernel(
    ids_row, route_row, tokens_in, cot_in, w_gate, w_up, w_down_in, spread, spread_t, place,
    token_out, route_out, grad_out,
    buf, back, ring, relay, back_relay, ret, w_nat, gu_wt, x_all, c_all, grads_all, grads_t, relay_in, relay_on,
    mirror_half, own_half, far_half, grad_in, grad_on, stack,
    w_sem, ag_send, ag_recv, y_send, y_recv, relay_send, relay_recv, r_send, r_recv, rs_send, rs_recv,
    m_send, m_recv, d_send, d_recv, c_send, c_recv,
):
    count, features = tokens_in.shape
    tokens, cot, w_down = (x_all.at[index * count : (index + 1) * count] for index in range(3))
    mirror_grad, own_grad = grad_out, gu_wt.at[0 : 3 * LANES]
    chunks = features // LANES
    pairs = chunks // 2
    half = features // 2
    direct = half // 2
    pieces = tuple((start, min(2 * LANES, half - start)) for start in range(direct, half, 2 * LANES))
    me_p = lax.axis_index("pipe")
    me_e = lax.axis_index("expert")
    plane = lax.div(me_p, 2)
    core = lax.rem(me_p, 2)
    y = lax.div(me_e, NZ)
    z = lax.rem(me_e, NZ)
    turn = lax.rem(y + 2 * plane, LINE)
    right = (me_p, y * NZ + lax.rem(z + 1, NZ))
    left = (me_p, y * NZ + lax.rem(z + NZ - 1, NZ))
    partner = (me_p + 1 - 2 * core, me_e)
    planes = lax.axis_size("pipe") // 2
    beside = tuple((2 * lax.rem(plane + apart, planes) + core, me_e) for apart in (1, planes - 1))
    mirror = (me_p, y * NZ + lax.rem(2 * turn + 7 - z + NZ, NZ))
    mirror_on = (me_p, y * NZ + lax.rem(2 * lax.rem(turn + 2, LINE) + 7 - z + NZ, NZ))
    ring_to = (right, left)
    base = core * half
    away = half - base

    def y_device(apart):
        return (me_p, lax.rem(y + apart, NY) * NZ + z)

    def position(q):
        return lax.rem(z + LINE - lax.rem(turn + q, LINE), LINE)

    def landed(q):
        return q + 3 - 3 * lax.div(3 - q, 3)

    def remote(source, target, send, recv, device):
        return pltpu.make_async_remote_copy(
            src_ref=source, dst_ref=target, send_sem=send, recv_sem=recv, device_id=device, device_id_type=MESH
        )

    def ag_copy(q, kind, way, slot):
        at = buf.at[q, kind, slot]
        return remote(at, at, ag_send.at[q, kind, way, slot], ag_recv.at[q, kind, slot], ring_to[way])

    def y_copy(q, kind, slot):
        return remote(buf.at[q, kind, slot], buf.at[q + 3, kind, slot], y_send.at[q, kind, slot], y_recv.at[q, kind, slot], y_device(q))

    def y_half(kind, slot):
        return remote(buf.at[2, kind, slot], relay.at[kind, slot], y_send.at[2, kind, slot], relay_recv.at[kind, slot], y_device(1 + 2 * kind))

    def y_rest(kind, slot):
        return remote(relay.at[kind, slot], buf.at[5, kind, slot], relay_send.at[kind, slot], y_recv.at[2, kind, slot], y_device(1 + 2 * kind))

    def r_half(slot):
        return remote(back.at[5, slot], back_relay.at[slot], r_send.at[2, slot], relay_recv.at[2, slot], y_device(1 + slot // 2 * 2))

    def r_rest(slot):
        return remote(back_relay.at[slot], back.at[2, slot], relay_send.at[2, slot], r_recv.at[2, slot], y_device(1 + slot // 2 * 2))

    def y_start(q, kind, slot):
        if q == 2:
            y_half(kind, slot).start()
        elif q > 0:
            y_copy(q, kind, slot).start()

    def relay_hop(hop):
        for kind in range(2):
            place_at = position(1 + 2 * kind)

            def onward(slot):
                y_half(kind, slot).wait_recv()
                y_rest(kind, slot).start()

            if hop == 0:
                onward(place_at)
                continue

            @pl.when(place_at >= hop)
            def _():
                onward(place_at - hop)

            @pl.when(place_at + hop < LINE)
            def _():
                onward(place_at + hop)

    def r_copy(q, slot):
        return remote(back.at[q + 3, slot], back.at[q, slot], r_send.at[q, slot], r_recv.at[q, slot], y_device(NY - q))

    def rs_copy(q, way, slot):
        return remote(back.at[q, slot], ring.at[q, way, slot - 1 + way], rs_send.at[q, way, slot], rs_recv.at[q, way, slot], ring_to[way])

    def rows_at(offset, size):
        return pl.ds(pl.multiple_of(base + offset, LANES), size)

    def weight_copy(leg, piece):
        if leg == 0:
            span = rows_at(0, direct)
            return remote(w_nat.at[0, span], w_nat.at[1, span], m_send.at[0], m_recv.at[0], mirror)
        offset, size = pieces[piece]
        span, local = rows_at(offset, size), pl.ds(offset - direct, size)
        number = len(pieces) * (leg - 1) + 1 + piece
        there, back_there = beside[piece % 2], beside[1 - piece % 2]
        if leg == 1:
            return remote(w_nat.at[0, span], relay_in.at[local], m_send.at[number], m_recv.at[number], there)
        if leg == 2:
            return remote(relay_in.at[local], relay_on.at[local], m_send.at[number], m_recv.at[number], mirror_on)
        return remote(relay_on.at[local], w_nat.at[1, span], m_send.at[number], m_recv.at[number], back_there)

    def grad_copy(leg, piece):
        if leg == 0:
            return remote(mirror_grad.at[:, rows_at(0, direct)], far_half.at[:, 0:direct], d_send.at[0], d_recv.at[0], mirror)
        offset, size = pieces[piece]
        span, local = rows_at(offset, size), pl.ds(offset - direct, size)
        number = len(pieces) * (leg - 1) + 1 + piece
        there, back_there = beside[piece % 2], beside[1 - piece % 2]
        if leg == 1:
            return remote(mirror_grad.at[:, span], grad_in.at[:, local], d_send.at[number], d_recv.at[number], there)
        if leg == 2:
            return remote(grad_in.at[:, local], grad_on.at[:, local], d_send.at[number], d_recv.at[number], mirror_on)
        return remote(grad_on.at[:, local], far_half.at[:, offset : offset + size], d_send.at[number], d_recv.at[number], back_there)

    def core_copy(number):
        if number < 2:
            span = rows_at(number * direct, direct)
            return remote(w_nat.at[1, span], w_nat.at[1, span], c_send.at[number], c_recv.at[number], partner)
        mine, other = rows_at(0, half), pl.ds(pl.multiple_of(away, LANES), half)
        if number == 2:
            return remote(mirror_grad.at[:, other], mirror_half, c_send.at[2], c_recv.at[2], partner)
        if number == 3:
            return remote(gu_wt.at[0 : 3 * LANES, other], own_half, c_send.at[3], c_recv.at[3], partner)
        return remote(grad_out.at[:, mine], grad_out.at[:, mine], c_send.at[4], c_recv.at[4], partner)

    def codes():
        rel = ids_row[...].astype(F32) - y.astype(F32)
        row = jnp.where(rel < 0, rel + NY, rel)
        first = lax.broadcasted_iota(jnp.int32, (count, count), 0)
        second = lax.broadcasted_iota(jnp.int32, (count, count), 1)
        col = to_column(row)
        same = jnp.where(col == row, 1.0, 0.0)
        slot_row = jnp.sum(jnp.where(first < second, same, 0.0), axis=0, keepdims=True)
        slot_col = jnp.sum(jnp.where(second < first, same, 0.0), axis=1, keepdims=True)
        code_row = jnp.where(slot_row < ROWS, row * ROWS + slot_row, MAIN + row)
        code_col = jnp.where(slot_col < ROWS, col * ROWS + slot_col, MAIN + col)
        return col, slot_col, code_row, code_col

    def to_column(row):
        first = lax.broadcasted_iota(jnp.int32, (count, count), 0)
        second = lax.broadcasted_iota(jnp.int32, (count, count), 1)
        return jnp.sum(jnp.where(first == second, row, 0.0), axis=1, keepdims=True)

    def one_hot(code, shape, dim, start=0):
        places = lax.broadcasted_iota(jnp.int32, shape, dim) + start
        return jnp.where(places.astype(F32) == code, 1.0, 0.0).astype(BF)

    def transposed(piece):
        for chunk in range(chunks):
            span = slice(chunk * LANES, (chunk + 1) * LANES)
            gu_wt[2 * LANES * piece : 2 * LANES * (piece + 1), span] = w_nat[piece, span, 0 : 2 * LANES].T

    loads = (
        pltpu.make_async_copy(w_gate, w_nat.at[0, :, 0:LANES], w_sem.at[0]),
        pltpu.make_async_copy(w_up, w_nat.at[0, :, LANES : 2 * LANES], w_sem.at[1]),
        pltpu.make_async_copy(w_down_in, w_down, w_sem.at[2]),
        pltpu.make_async_copy(tokens_in, tokens, w_sem.at[3]),
        pltpu.make_async_copy(cot_in, cot, w_sem.at[4]),
    )
    for copy in loads:
        copy.start()
    barrier = pltpu.get_barrier_semaphore()
    for device in (right, left, y_device(1), y_device(2), y_device(3), partner) + beside + (mirror, mirror_on):
        pl.semaphore_signal(barrier, inc=1, device_id=device, device_id_type=MESH)
    loads[2].wait()
    for chunk in range(chunks):
        span = slice(chunk * LANES, (chunk + 1) * LANES)
        w_nat[0, span, 2 * LANES : 3 * LANES] = w_down[:, span].T
    for index in (0, 1, 3, 4):
        loads[index].wait()
    pl.semaphore_wait(barrier, 10)
    for piece in range(len(pieces)):
        weight_copy(1, piece).start()
    weight_copy(0, 0).start()

    def own_start(q, kind):
        place_at = position(q)

        @pl.when(place_at < LINE - 1)
        def _():
            ag_copy(q, kind, 0, place_at).start()

        @pl.when(place_at > 0)
        def _():
            ag_copy(q, kind, 1, place_at).start()

        y_start(q, kind, place_at)

    _, _, code_row, _ = codes()
    pick = one_hot(code_row, (QROWS, count), 0)
    c_all[0:count] = (cot[...].astype(F32) * to_column(route_row[...].astype(F32))).astype(BF)
    for kind, values in ((0, tokens), (1, c_all)):
        for pair in range(pairs):
            rows = dot(pick, values[0:count, 2 * LANES * pair : 2 * LANES * (pair + 1)]).astype(BF)
            for side in range(2):
                chunk = 2 * pair + side
                part = rows[:, side * LANES : (side + 1) * LANES]
                for q in range(NY):
                    buf[q, kind, position(q), chunk] = part[q * ROWS : (q + 1) * ROWS]
                stack[chunk * FOLD : (chunk + 1) * FOLD] = part[MAIN:QROWS]
        folded = dot(spread_t[...], stack[...]).astype(BF)
        for q in range(NY):
            buf[q, kind, position(q), chunks] = folded[q * ROWS : (q + 1) * ROWS]
        for q in (2, 1, 3, 0):
            own_start(q, kind)

    def gather_hop(q, hop):
        place_at = position(q)

        def one_kind(kind, carry):
            def arrived(way, slot, onward):
                ag_copy(q, kind, way, slot).wait_recv()

                @pl.when(onward)
                def _():
                    ag_copy(q, kind, way, slot).start()

                y_start(q, kind, slot)

            @pl.when(place_at >= hop)
            def _():
                arrived(0, place_at - hop, place_at < LINE - 1)

            @pl.when(place_at + hop < LINE)
            def _():
                arrived(1, place_at + hop, place_at > 0)

            return carry

        lax.fori_loop(0, 2, one_kind, 0)

    def merge(first, second):
        total = first.astype(F32) + second.astype(F32)
        sums = total[HIGH : HIGH + 1] + total[LOW : LOW + 1]
        high = sums.astype(BF).astype(F32)
        row = lax.broadcasted_iota(jnp.int32, (ROWS, LANES), 0)
        return jnp.where(row == HIGH, high, jnp.where(row == LOW, sums - high, total)).astype(BF)

    def add_message(target, first, second):
        target[0:chunks] = (first[0:chunks].astype(F32) + second[0:chunks].astype(F32)).astype(BF)
        target[chunks] = merge(first[chunks], second[chunks])

    def reduce_level(q, level):
        place_at = position(q)

        def step(way, slot, came):
            if level > 0:
                rs_copy(q, way, slot).wait_recv()
                add_message(back.at[q, slot], back.at[q, slot], ring.at[q, way, came])
            rs_copy(q, way, slot).start()

        @pl.when(place_at == level)
        def _():
            for slot in range(LINE - 1, level, -1):
                step(0, slot, slot - 1)

        @pl.when(place_at == LINE - 1 - level)
        def _():
            for slot in range(LINE - 1 - level):
                step(1, slot, slot)

    def reduce_end(q):
        place_at = position(q)
        ret[q] = back[q, place_at]

        @pl.when(place_at > 0)
        def _():
            rs_copy(q, 0, place_at).wait_recv()
            add_message(ret.at[q], ret.at[q], ring.at[q, 0, place_at - 1])

        @pl.when(place_at < LINE - 1)
        def _():
            rs_copy(q, 1, place_at).wait_recv()
            add_message(ret.at[q], ret.at[q], ring.at[q, 1, place_at])

    def returned(q):
        for slot in range(LINE):
            r_copy(q, slot).wait_recv()

    def compute_rows(q):
        at = landed(q)
        start = q * QROWS
        block = pl.ds(pl.multiple_of(start, FOLD), QROWS)
        for kind, rows in ((0, x_all), (1, c_all)):
            folded = buf[at, kind, :, chunks].reshape(MAIN, LANES)
            unfolded = dot(spread[...], folded).astype(BF)
            for chunk in range(chunks):
                span = slice(chunk * LANES, (chunk + 1) * LANES)
                rows[pl.ds(pl.multiple_of(start, FOLD), MAIN), span] = buf[at, kind, :, chunk].reshape(MAIN, LANES)
                rows[pl.ds(pl.multiple_of(start + MAIN, FOLD), FOLD), span] = unfolded[chunk * FOLD : (chunk + 1) * FOLD]
        slot = jnp.zeros((QROWS, 1), F32)
        both = []
        for piece in range(2):
            pre = dot(x_all[block], w_nat[piece, :, 0 : 2 * LANES])
            gate, up = pre[:, 0:LANES], pre[:, LANES : 2 * LANES]
            hidden_grad = dot(c_all[block], w_nat[piece, :, 2 * LANES : 3 * LANES])
            sig = jax.nn.sigmoid(gate)
            hidden = (gate * sig * up).astype(BF)
            grad_gate = (hidden_grad * up * sig * (1.0 + gate * (1.0 - sig))).astype(BF)
            grad_up = (hidden_grad * gate * sig).astype(BF)
            first = 3 * LANES * piece
            grads_all[block, first : first + LANES] = grad_gate
            grads_all[block, first + LANES : first + 2 * LANES] = grad_up
            grads_all[block, first + 2 * LANES : first + 3 * LANES] = hidden
            both += [grad_gate, grad_up]
            slot = slot + jnp.sum(hidden.astype(F32) * hidden_grad, axis=1, keepdims=True)
        grads = jnp.concatenate(both, axis=1)
        for pair in range(pairs):
            rows = dot(grads, gu_wt[:, 2 * LANES * pair : 2 * LANES * (pair + 1)]).astype(BF)
            for side in range(2):
                chunk = 2 * pair + side
                part = rows[:, side * LANES : (side + 1) * LANES]
                back[at, :, chunk] = part[0:MAIN].reshape(LINE, ROWS, LANES)
                stack[chunk * FOLD : (chunk + 1) * FOLD] = part[MAIN:QROWS]
        which = lax.broadcasted_iota(jnp.int32, (QROWS, LANES), 0)
        lane = lax.broadcasted_iota(jnp.int32, (QROWS, LANES), 1)
        wanted = jnp.where(which < MAIN, lax.rem(which, ROWS), ROWS)
        spots = jnp.where(lane == wanted, slot, 0.0)
        high = spots.astype(BF)
        low = (spots - high.astype(F32)).astype(BF)
        folded = dot(spread_t[...], stack[...]) + dot(place[0], high) + dot(place[1], low)
        back[at, :, chunks] = folded.astype(BF).reshape(LINE, ROWS, LANES)

    transposed(0)
    for piece in range(len(pieces)):
        weight_copy(1, piece).wait_recv()
        weight_copy(2, piece).start()
    relay_hop(0)
    for q in (2, 1, 3, 0):
        gather_hop(q, 1)
    for piece in range(len(pieces)):
        weight_copy(2, piece).wait_recv()
        weight_copy(3, piece).start()
    relay_hop(1)
    for q in (2, 1, 3, 0):
        gather_hop(q, 2)
    weight_copy(0, 0).wait_recv()
    core_copy(0).start()
    for piece in range(len(pieces)):
        weight_copy(3, piece).wait_recv()
    core_copy(1).start()
    relay_hop(2)
    for q in (2, 1, 3, 0):
        gather_hop(q, 3)
    for number in range(2):
        core_copy(number).wait_recv()
    transposed(1)
    relay_hop(3)

    def quarter(step, carry):
        q = step + lax.div(step, 2) * (5 - 2 * step)

        @pl.when(q > 0)
        def _():
            for kind in range(2):
                for slot in range(LINE):
                    y_copy(q, kind, slot).wait_recv()

        compute_rows(q)

        @pl.when(step == 0)
        def _():
            reduce_level(0, 0)

        @pl.when((step == 1) | (step == 2))
        def _():
            for slot in range(LINE):
                r_copy(q, slot).start()

        @pl.when(step == 3)
        def _():
            for slot in range(LINE):
                r_half(slot).start()

        @pl.when(step == 1)
        def _():
            reduce_level(0, 1)

        @pl.when(step == 2)
        def _():
            returned(1)
            reduce_level(1, 0)
            reduce_level(0, 2)

        @pl.when(step == 3)
        def _():
            returned(3)
            reduce_level(3, 0)
            reduce_level(1, 1)

        return carry

    lax.fori_loop(0, NY, quarter, 0)

    width = 4 * LANES
    grads_t[...] = grads_all[...].T

    def weight_terms(piece, target):
        first = 3 * LANES * piece
        for start in range(0, features, width):
            span = slice(start, start + width)
            target[0 : 2 * LANES, span] = dot(grads_t[first : first + 2 * LANES], x_all[:, span]).astype(BF)
            target[2 * LANES : 3 * LANES, span] = dot(grads_t[first + 2 * LANES : first + 3 * LANES], c_all[:, span]).astype(BF)

    weight_terms(1, mirror_grad)
    core_copy(2).start()
    for slot in range(LINE):
        r_half(slot).wait_recv()
        r_rest(slot).start()
    reduce_level(1, 2)
    reduce_level(3, 1)
    core_copy(2).wait_recv()
    mine = rows_at(0, half)
    mirror_grad[:, mine] = (mirror_grad[:, mine].astype(F32) + mirror_half[...].astype(F32)).astype(BF)
    for piece in range(len(pieces)):
        grad_copy(1, piece).start()
    grad_copy(0, 0).start()
    returned(2)
    reduce_level(2, 0)
    weight_terms(0, own_grad)
    core_copy(2).wait_send()
    core_copy(3).start()
    reduce_level(3, 2)
    for piece in range(len(pieces)):
        grad_copy(1, piece).wait_recv()
        grad_copy(2, piece).start()
    reduce_level(2, 1)
    for q in (0, 1):
        reduce_end(q)
    reduce_level(2, 2)
    for piece in range(len(pieces)):
        grad_copy(2, piece).wait_recv()
        grad_copy(3, piece).start()
    for q in (3, 2):
        reduce_end(q)

    col, slot_col, _, code_col = codes()
    unpick = one_hot(code_col, (count, MAIN), 1)
    unpick_fold = one_hot(code_col, (count, FOLD), 1, MAIN)
    folded = ret[:, chunks].reshape(MAIN, LANES)
    unfolded = dot(spread[...], folded).astype(BF)
    for chunk in range(chunks):
        rows = ret[:, chunk].reshape(MAIN, LANES)
        total = dot(unpick, rows) + dot(unpick_fold, unfolded[chunk * FOLD : (chunk + 1) * FOLD])
        token_out[:, chunk * LANES : (chunk + 1) * LANES] = total.astype(BF)
    lane = lax.broadcasted_iota(jnp.int32, (count, LANES), 1).astype(F32)
    total = jnp.zeros((count, LANES), F32)
    for q in range(NY):
        last = ret[q, chunks].astype(F32)
        entry = last[HIGH : HIGH + 1] + last[LOW : LOW + 1]
        total = total + jnp.where((lane == slot_col) & (col == q), entry, 0.0)
    slot_sum = jnp.sum(total, axis=1, keepdims=True)
    first = lax.broadcasted_iota(jnp.int32, (count, count), 0)
    second = lax.broadcasted_iota(jnp.int32, (count, count), 1)
    sum_row = jnp.sum(jnp.where(first == second, slot_sum, 0.0), axis=0, keepdims=True)
    route_out[...] = (sum_row / route_row[...].astype(F32)).astype(BF)

    core_copy(3).wait_recv()
    grad_copy(0, 0).wait_recv()
    for piece in range(len(pieces)):
        grad_copy(3, piece).wait_recv()
    grad_copy(0, 0).wait_send()
    for piece in range(len(pieces)):
        grad_copy(1, piece).wait_send()
    grad_out[:, mine] = (own_grad[:, mine].astype(F32) + own_half[...].astype(F32) + far_half[...].astype(F32)).astype(BF)
    core_copy(4).start()
    core_copy(4).wait_recv()

    for number in (0, 1, 3, 4):
        core_copy(number).wait_send()
    weight_copy(0, 0).wait_send()
    for piece in range(len(pieces)):
        weight_copy(1, piece).wait_send()
        for leg in (2, 3):
            weight_copy(leg, piece).wait_send()
            grad_copy(leg, piece).wait_send()
    for q in range(NY):
        place_at = position(q)
        for slot in range(LINE):
            for kind in range(2):
                if q > 0:
                    y_copy(q, kind, slot).wait_send()

                @pl.when((slot <= place_at) & (place_at < LINE - 1))
                def _():
                    ag_copy(q, kind, 0, slot).wait_send()

                @pl.when((slot >= place_at) & (place_at > 0))
                def _():
                    ag_copy(q, kind, 1, slot).wait_send()

            if q > 0:
                r_copy(q, slot).wait_send()
            if q < 2:
                y_rest(q, slot).wait_send()
            if q == 2:
                r_rest(slot).wait_send()
            if slot > 0:

                @pl.when(place_at < slot)
                def _():
                    rs_copy(q, 0, slot).wait_send()

            if slot < LINE - 1:

                @pl.when(place_at > slot)
                def _():
                    rs_copy(q, 1, slot).wait_send()


def shards(tokens, expert_ids, route_weight, cotangent, w_gate, w_up, w_down):
    count, features = tokens.shape[1:]
    hidden = w_gate.shape[2]
    chunks = features // LANES
    spread, spread_t, place = fold_matrices(chunks)
    vmem = pl.BlockSpec(memory_space=pltpu.VMEM)
    anywhere = pl.BlockSpec(memory_space=pl.ANY)
    message = (chunks + 1, ROWS, LANES)
    half = features // 2
    dma = pltpu.SemaphoreType.DMA
    token_grad, route_grad, weight_grad = pl.pallas_call(
        kernel,
        out_shape=(
            jax.ShapeDtypeStruct((count, features), BF),
            jax.ShapeDtypeStruct((1, count), BF),
            jax.ShapeDtypeStruct((3 * hidden, features), BF),
        ),
        in_specs=[vmem] * 2 + [anywhere] * 5 + [vmem] * 3,
        out_specs=(vmem, vmem, vmem),
        scratch_shapes=[
            pltpu.VMEM((7, 2, LINE) + message, BF),
            pltpu.VMEM((7, LINE) + message, BF),
            pltpu.VMEM((NY, 2, LINE - 1) + message, BF),
            pltpu.VMEM((2, LINE) + message, BF),
            pltpu.VMEM((LINE,) + message, BF),
            pltpu.VMEM((NY,) + message, BF),
            pltpu.VMEM((2, features, 3 * hidden), BF),
            pltpu.VMEM((4 * hidden, features), BF),
            pltpu.VMEM((NY * QROWS, features), BF),
            pltpu.VMEM((NY * QROWS, features), BF),
            pltpu.VMEM((NY * QROWS, 6 * hidden), BF),
            pltpu.VMEM((6 * hidden, NY * QROWS), BF),
            pltpu.VMEM((half // 2, 3 * hidden), BF),
            pltpu.VMEM((half // 2, 3 * hidden), BF),
            pltpu.VMEM((3 * hidden, half), BF),
            pltpu.VMEM((3 * hidden, half), BF),
            pltpu.VMEM((3 * hidden, half), BF),
            pltpu.VMEM((3 * hidden, half // 2), BF),
            pltpu.VMEM((3 * hidden, half // 2), BF),
            pltpu.VMEM((chunks * FOLD, LANES), BF),
            dma((5,)),
            dma((NY, 2, 2, LINE)),
            dma((NY, 2, LINE)),
            dma((NY, 2, LINE)),
            dma((NY, 2, LINE)),
            dma((3, LINE)),
            dma((3, LINE)),
            dma((NY, LINE)),
            dma((NY, LINE)),
            dma((NY, 2, LINE)),
            dma((NY, 2, LINE)),
            dma((13,)),
            dma((13,)),
            dma((13,)),
            dma((13,)),
            dma((5,)),
            dma((5,)),
        ],
        compiler_params=pltpu.CompilerParams(
            collective_id=0, has_side_effects=True, vmem_limit_bytes=63 * 1024 * 1024
        ),
        cost_estimate=pl.CostEstimate(flops=8_000_000_000, bytes_accessed=10_000_000, transcendentals=140_000),
    )(
        expert_ids.reshape(1, count), route_weight.reshape(1, count), tokens[0], cotangent[0],
        w_gate[0], w_up[0], w_down[0], spread, spread_t, place,
    )
    grad_gate = weight_grad[0:hidden].T
    grad_up = weight_grad[hidden : 2 * hidden].T
    grad_down = weight_grad[2 * hidden : 3 * hidden]
    return (token_grad[None], route_grad.reshape(1, count, 1), grad_gate[None], grad_up[None], grad_down[None])


def solution(mesh):
    rows = P("pipe", "expert", None)
    columns = P("pipe", None, "expert")
    return jax.shard_map(
        shards, mesh=mesh,
        in_specs=(rows, rows, rows, rows, columns, columns, rows),
        out_specs=(rows, rows, columns, columns, rows),
        check_vma=False,
    )
```

time: 777 us -> 237 us (0.31)
  waiting for transfers between devices: 372 us -> 0 us
  Pallas kernels: 0 us -> 228 us
  blocking collectives: 212 us -> 0 us
  local copies, waits for them, and re-layouts: 67.9 us -> 6.8 us
  matrix products: 50.4 us -> 0 us
  starting transfers between devices: 34.9 us -> 0 us
  other arithmetic: 31.8 us -> 0 us
    all_to_all x4 -> x0, waiting for transfers between devices: 372 us -> none  [the longest x1 188 us: shards(): lax.all_to_all(row_grad.reshape(devices_count, capacity, feature_count),...]
    pallas_call x0 -> x1, Pallas kernels: none -> 228 us  [shards(): pl.pallas_call(kernel, out_shape=(jax.ShapeDtypeStruct((count, features),...]
    all_to_all x1 -> x0, blocking collectives: 212 us -> none  [shards(): lax.all_to_all(cot_send, 'expert', split_axis=0, concat_axis=0, tiled=True)]
    dot_general x9 -> x0, matrix products: 50.4 us -> none  [the longest x3 18.8 us: contract_rows(): lax.dot_general(left, right, (((0,), (0,)), ((), ())), preferred_element_...]
    all_to_all x4 -> x0, starting transfers between devices: 34 us -> none  [the longest x1 11.4 us: shards(): lax.all_to_all(weight_send, 'expert', split_axis=0, concat_axis=0, tiled=...]
    reshape x5 -> x0, local copies, waits for them, and re-layouts: 24.9 us -> none  [the longest x1 8.97 us: shards(): grouped = back_rows.reshape(EXPERTS, group_size, capacity, feature_count)]
    convert_element_type x4 -> x0, local copies, waits for them, and re-layouts: 19 us -> none  [the longest x1 10.2 us: expert_backward(): cot_wide = cot_rows.astype(jnp.float32)]
    gather x7 -> x0, local copies, waits for them, and re-layouts: 17.3 us -> none  [the longest x4 7.13 us: pack_rows(): picked = values[jnp.maximum(source_row, 0) // top_count]]
  transfers between devices with their start and end apart: 7 -> 0, of which waited for: 2 -> 0; matrix products, arithmetic and copies ran while one was open for 10% -> 0% of each run, Pallas kernels for 0% -> 0%
where the time goes in v3:
time: 237 us; the launch traced here: 236 us
  Pallas kernels  228 us (96%)
  local copies, waits for them, and re-layouts  6.8 us (3%)
    pallas_call x1, Pallas kernels, shards(): pl.pallas_call(kernel, out_shape=(jax.ShapeDtypeStruct((count, features),...  228 us

profile of v3, /device:TPU:32, one launch (start us, length us, event | category | flops | bytes accessed | tf_op | source)
XLA Modules:
  0.0 235.7 jit_solution(8459354351636482243)
XLA Ops:
  0.6 228.3 %shard_map.137 = (bf16[128,3584]{1,0:T(8,128)(2,1)}, bf16[1,128]{1,0:T(2,128)(2,1)}, bf16[384,3584]{1,0:T(8,128)(2,1)}) custom-call(s32[1,128]{1,0:T(1,128)} %bitcast.25, bf16[1,128]{1,0:T(2,128)(2,1)} %bitcast.26, bf16[128,3584]{1,0:T(8,128)(2,1)} %bitcast.20, bf16[128,3584]{1,0:T(8,128)(2,1)} %bitcast.21, bf16[3584,128]{1,0:T(8,128)(2,1)} %bitcast.22, ...), custom_call_target="tpu_custom_call" | custom-call | flops 8000000000 | bytes 10000000 | tf_op jit(solution)/shard_map/pallas_call | solution.py:573
  228.9 2.8 %slice_bitcast_fusion = (bf16[1,128,3584]{2,1,0:T(8,128)(2,1)}, bf16[1,3584,128]{1,2,0:T(8,128)(2,1)S(1)}, bf16[1,3584,128]{1,2,0:T(8,128)(2,1)S(1)}) fusion(bf16[384,3584]{1,0:T(8,128)(2,1)} %get-tuple-element.10), kind=kLoop, calls=%fused_computation | loop fusion | bytes 5505024 | tf_op jit(solution)/shard_map/broadcast_in_dim | solution.py:632
  231.7 0.0 copy-start
  231.7 0.0 copy-start.1
  231.7 1.3 copy.16
  233.0 1.3 copy.15
  234.3 0.0 copy-done
  234.3 0.9 copy.19
  235.2 0.0 copy-done.1
  235.2 0.5 copy.20
Async XLA Ops:
  231.7 2.5 %copy-start = (bf16[128,3584]{1,0:T(8,128)(2,1)S(1)}, bf16[128,3584]{1,0:T(8,128)(2,1)}, u32[]{:S(2)}) copy-start(bf16[128,3584]{1,0:T(8,128)(2,1)} %get-tuple-element.8) | copy-start | bytes 2752516
  231.7 3.5 %copy-start.1 = (bf16[1,128]{1,0:T(2,128)(2,1)S(1)}, bf16[1,128]{1,0:T(2,128)(2,1)}, u32[]{:S(2)}) copy-start(bf16[1,128]{1,0:T(2,128)(2,1)} %get-tuple-element.9) | copy-start | bytes 772

commit v4 on v3

--- a/solution.py
+++ b/solution.py
@@ -50,7 +50,9 @@
     pairs = chunks // 2
     half = features // 2
     direct = half // 2
+    direct_back = direct
     pieces = tuple((start, min(2 * LANES, half - start)) for start in range(direct, half, 2 * LANES))
+    pieces_back = tuple((start, min(2 * LANES, half - start)) for start in range(direct_back, half, 2 * LANES))
     me_p = lax.axis_index("pipe")
     me_e = lax.axis_index("expert")
     plane = lax.div(me_p, 2)
@@ -153,10 +155,10 @@
 
     def grad_copy(leg, piece):
         if leg == 0:
-            return remote(mirror_grad.at[:, rows_at(0, direct)], far_half.at[:, 0:direct], d_send.at[0], d_recv.at[0], mirror)
-        offset, size = pieces[piece]
-        span, local = rows_at(offset, size), pl.ds(offset - direct, size)
-        number = len(pieces) * (leg - 1) + 1 + piece
+            return remote(mirror_grad.at[:, rows_at(0, direct_back)], far_half.at[:, 0:direct_back], d_send.at[0], d_recv.at[0], mirror)
+        offset, size = pieces_back[piece]
+        span, local = rows_at(offset, size), pl.ds(offset - direct_back, size)
+        number = len(pieces_back) * (leg - 1) + 1 + piece
         there, back_there = beside[piece % 2], beside[1 - piece % 2]
         if leg == 1:
             return remote(mirror_grad.at[:, span], grad_in.at[:, local], d_send.at[number], d_recv.at[number], there)
@@ -209,22 +211,11 @@
         pltpu.make_async_copy(tokens_in, tokens, w_sem.at[3]),
         pltpu.make_async_copy(cot_in, cot, w_sem.at[4]),
     )
-    for copy in loads:
-        copy.start()
+    for index in (3, 4, 2, 0, 1):
+        loads[index].start()
     barrier = pltpu.get_barrier_semaphore()
     for device in (right, left, y_device(1), y_device(2), y_device(3), partner) + beside + (mirror, mirror_on):
         pl.semaphore_signal(barrier, inc=1, device_id=device, device_id_type=MESH)
-    loads[2].wait()
-    for chunk in range(chunks):
-        span = slice(chunk * LANES, (chunk + 1) * LANES)
-        w_nat[0, span, 2 * LANES : 3 * LANES] = w_down[:, span].T
-    for index in (0, 1, 3, 4):
-        loads[index].wait()
-    pl.semaphore_wait(barrier, 10)
-    for piece in range(len(pieces)):
-        weight_copy(1, piece).start()
-    weight_copy(0, 0).start()
-
     def own_start(q, kind):
         place_at = position(q)
 
@@ -240,8 +231,11 @@
 
     _, _, code_row, _ = codes()
     pick = one_hot(code_row, (QROWS, count), 0)
-    c_all[0:count] = (cot[...].astype(F32) * to_column(route_row[...].astype(F32))).astype(BF)
+    loads[3].wait()
     for kind, values in ((0, tokens), (1, c_all)):
+        if kind == 1:
+            loads[4].wait()
+            c_all[0:count] = (cot[...].astype(F32) * to_column(route_row[...].astype(F32))).astype(BF)
         for pair in range(pairs):
             rows = dot(pick, values[0:count, 2 * LANES * pair : 2 * LANES * (pair + 1)]).astype(BF)
             for side in range(2):
@@ -253,8 +247,18 @@
         folded = dot(spread_t[...], stack[...]).astype(BF)
         for q in range(NY):
             buf[q, kind, position(q), chunks] = folded[q * ROWS : (q + 1) * ROWS]
+        if kind == 0:
+            pl.semaphore_wait(barrier, 10)
         for q in (2, 1, 3, 0):
             own_start(q, kind)
+    loads[2].wait()
+    for chunk in range(chunks):
+        span = slice(chunk * LANES, (chunk + 1) * LANES)
+        w_nat[0, span, 2 * LANES : 3 * LANES] = w_down[:, span].T
+    for index in (0, 1):
+        loads[index].wait()
+    for piece in range(len(pieces)):
+        weight_copy(1, piece).start()
 
     def gather_hop(q, hop):
         place_at = position(q)
@@ -374,30 +378,31 @@
         back[at, :, chunks] = folded.astype(BF).reshape(LINE, ROWS, LANES)
 
     transposed(0)
+    relay_hop(0)
+    for q in (2, 1, 3, 0):
+        gather_hop(q, 1)
+    relay_hop(1)
+    for q in (2, 1, 3, 0):
+        gather_hop(q, 2)
+    weight_copy(0, 0).start()
     for piece in range(len(pieces)):
         weight_copy(1, piece).wait_recv()
         weight_copy(2, piece).start()
-    relay_hop(0)
+    relay_hop(2)
     for q in (2, 1, 3, 0):
-        gather_hop(q, 1)
+        gather_hop(q, 3)
     for piece in range(len(pieces)):
         weight_copy(2, piece).wait_recv()
         weight_copy(3, piece).start()
-    relay_hop(1)
-    for q in (2, 1, 3, 0):
-        gather_hop(q, 2)
+    relay_hop(3)
     weight_copy(0, 0).wait_recv()
     core_copy(0).start()
     for piece in range(len(pieces)):
         weight_copy(3, piece).wait_recv()
     core_copy(1).start()
-    relay_hop(2)
-    for q in (2, 1, 3, 0):
-        gather_hop(q, 3)
     for number in range(2):
         core_copy(number).wait_recv()
     transposed(1)
-    relay_hop(3)
 
     def quarter(step, carry):
         q = step + lax.div(step, 2) * (5 - 2 * step)
@@ -444,43 +449,42 @@
 
     lax.fori_loop(0, NY, quarter, 0)
 
-    width = 4 * LANES
     grads_t[...] = grads_all[...].T
 
     def weight_terms(piece, target):
         first = 3 * LANES * piece
-        for start in range(0, features, width):
-            span = slice(start, start + width)
+        for start in range(0, features, 4 * LANES):
+            span = slice(start, start + 4 * LANES)
             target[0 : 2 * LANES, span] = dot(grads_t[first : first + 2 * LANES], x_all[:, span]).astype(BF)
             target[2 * LANES : 3 * LANES, span] = dot(grads_t[first + 2 * LANES : first + 3 * LANES], c_all[:, span]).astype(BF)
 
     weight_terms(1, mirror_grad)
     core_copy(2).start()
-    for slot in range(LINE):
-        r_half(slot).wait_recv()
-        r_rest(slot).start()
     reduce_level(1, 2)
     reduce_level(3, 1)
     core_copy(2).wait_recv()
     mine = rows_at(0, half)
-    mirror_grad[:, mine] = (mirror_grad[:, mine].astype(F32) + mirror_half[...].astype(F32)).astype(BF)
-    for piece in range(len(pieces)):
-        grad_copy(1, piece).start()
-    grad_copy(0, 0).start()
-    returned(2)
-    reduce_level(2, 0)
+    for piece, (offset, size) in enumerate(pieces_back + ((0, direct_back),)):
+        span = rows_at(offset, size)
+        mirror_grad[:, span] = (mirror_grad[:, span].astype(F32) + mirror_half[:, offset : offset + size].astype(F32)).astype(BF)
+        grad_copy(*((1, piece) if offset else (0, 0))).start()
+    for slot in range(LINE):
+        r_half(slot).wait_recv()
+        r_rest(slot).start()
     weight_terms(0, own_grad)
     core_copy(2).wait_send()
     core_copy(3).start()
-    reduce_level(3, 2)
-    for piece in range(len(pieces)):
+    for piece in range(len(pieces_back)):
         grad_copy(1, piece).wait_recv()
         grad_copy(2, piece).start()
+    returned(2)
+    reduce_level(2, 0)
+    reduce_level(3, 2)
     reduce_level(2, 1)
     for q in (0, 1):
         reduce_end(q)
     reduce_level(2, 2)
-    for piece in range(len(pieces)):
+    for piece in range(len(pieces_back)):
         grad_copy(2, piece).wait_recv()
         grad_copy(3, piece).start()
     for q in (3, 2):
@@ -509,10 +513,10 @@
 
     core_copy(3).wait_recv()
     grad_copy(0, 0).wait_recv()
-    for piece in range(len(pieces)):
+    for piece in range(len(pieces_back)):
         grad_copy(3, piece).wait_recv()
     grad_copy(0, 0).wait_send()
-    for piece in range(len(pieces)):
+    for piece in range(len(pieces_back)):
         grad_copy(1, piece).wait_send()
     grad_out[:, mine] = (own_grad[:, mine].astype(F32) + own_half[...].astype(F32) + far_half[...].astype(F32)).astype(BF)
     core_copy(4).start()
@@ -521,10 +525,11 @@
     for number in (0, 1, 3, 4):
         core_copy(number).wait_send()
     weight_copy(0, 0).wait_send()
-    for piece in range(len(pieces)):
-        weight_copy(1, piece).wait_send()
-        for leg in (2, 3):
+    for leg in (1, 2, 3):
+        for piece in range(len(pieces)):
             weight_copy(leg, piece).wait_send()
+    for leg in (2, 3):
+        for piece in range(len(pieces_back)):
             grad_copy(leg, piece).wait_send()
     for q in range(NY):
         place_at = position(q)

time: 237 us -> 225 us (0.949)
  Pallas kernels: 228 us -> 215 us
    pallas_call x1, Pallas kernels: 228 us -> 215 us  [shards(): pl.pallas_call(kernel, out_shape=(jax.ShapeDtypeStruct((count, features),...]
where the time goes in v4:
time: 225 us; the launch traced here: 223 us
  Pallas kernels  215 us (96%)
  local copies, waits for them, and re-layouts  6.8 us (3%)
    pallas_call x1, Pallas kernels, shards(): pl.pallas_call(kernel, out_shape=(jax.ShapeDtypeStruct((count, features),...  215 us

profile of v4, /device:TPU:32, one launch (start us, length us, event | category | flops | bytes accessed | tf_op | source)
XLA Modules:
  0.0 222.7 jit_solution(2096272284007580860)
XLA Ops:
  0.6 215.2 %shard_map.137 = (bf16[128,3584]{1,0:T(8,128)(2,1)}, bf16[1,128]{1,0:T(2,128)(2,1)}, bf16[384,3584]{1,0:T(8,128)(2,1)}) custom-call(s32[1,128]{1,0:T(1,128)} %bitcast.25, bf16[1,128]{1,0:T(2,128)(2,1)} %bitcast.26, bf16[128,3584]{1,0:T(8,128)(2,1)} %bitcast.20, bf16[128,3584]{1,0:T(8,128)(2,1)} %bitcast.21, bf16[3584,128]{1,0:T(8,128)(2,1)} %bitcast.22, ...), custom_call_target="tpu_custom_call" | custom-call | flops 8000000000 | bytes 10000000 | tf_op jit(solution)/shard_map/pallas_call | solution.py:578
  215.9 2.8 %slice_bitcast_fusion = (bf16[1,128,3584]{2,1,0:T(8,128)(2,1)}, bf16[1,3584,128]{1,2,0:T(8,128)(2,1)S(1)}, bf16[1,3584,128]{1,2,0:T(8,128)(2,1)S(1)}) fusion(bf16[384,3584]{1,0:T(8,128)(2,1)} %get-tuple-element.10), kind=kLoop, calls=%fused_computation | loop fusion | bytes 5505024 | tf_op jit(solution)/shard_map/broadcast_in_dim | solution.py:637
  218.7 0.0 copy-start
  218.7 0.0 copy-start.1
  218.7 1.3 copy.16
  220.0 1.3 copy.15
  221.2 0.0 copy-done
  221.3 0.9 copy.19
  222.2 0.0 copy-done.1
  222.2 0.5 copy.20
Async XLA Ops:
  218.7 2.5 %copy-start = (bf16[128,3584]{1,0:T(8,128)(2,1)S(1)}, bf16[128,3584]{1,0:T(8,128)(2,1)}, u32[]{:S(2)}) copy-start(bf16[128,3584]{1,0:T(8,128)(2,1)} %get-tuple-element.8) | copy-start | bytes 2752516
  218.7 3.5 %copy-start.1 = (bf16[1,128]{1,0:T(2,128)(2,1)S(1)}, bf16[1,128]{1,0:T(2,128)(2,1)}, u32[]{:S(2)}) copy-start(bf16[1,128]{1,0:T(2,128)(2,1)} %get-tuple-element.9) | copy-start | bytes 772
